TPU v7x, 256 devices: a whole 4x4x8 slice. The times are simulated.
256 devices in a mesh: ctx: 32 (over y_lo, z, core), head: 8 (over x, y_hi).
Axes of the slice: x: 4, y: 4 (y_hi: 2, y_lo: 2; y = y_hi * 2 + y_lo), z: 8, core: 2. Of those that a mesh axis runs over, the one named last changes fastest.
Arguments:
- queries: bfloat16 [2, 6144, 8192], P(None, 'ctx', 'head'), may hold values from -10 to 10
- key_states: bfloat16 [2, 6144, 1024], P(None, 'ctx', 'head'), may hold values from -6 to 6
- value_states: bfloat16 [2, 6144, 1024], P(None, 'ctx', 'head'), may hold values from -6 to 6
- segment_ids: int32 [12288], replicated, may hold values from 0 to 3, never falling along the last dimension, each value on 1 to 6144 neighbouring positions
Outputs:
- attended: bfloat16 [2, 6144, 8192], P(None, 'ctx', 'head')
- key_cache: bfloat16 [12288, 1024], P(('ctx', 'head'))
- value_cache: bfloat16 [12288, 1024], P(('ctx', 'head'))
Inputs may be any that keep to these rules, and one draw needn't show every extreme that they name: `segment_ids`: segment numbers never fall along positions; each segment spans 1 to 6144 positions, and one spans exactly 6144.
All inputs are finite; a program needn't handle non-finite values.
Results may differ from a plain program's by a relative error of at most 0.0055.
Values may be sent and summed in bfloat16 or wider, within the bound.
A program may use at most 64 MiB of HBM per device.

v0:
```python
from functools import partial
import math

import jax
import jax.numpy as jnp
from jax import lax
from jax.sharding import PartitionSpec as P

DH = 128


masked_score = -1e30


def partner(x, axis, distance):
    return lax.ppermute(x, axis, [(i, i ^ 1 << distance) for i in range(lax.axis_size(axis))])


def keep_state(carried):
    return carried


def attend_block(
    carried,
    query_stretch,
    query_segs,
    query_first,
    key_block,
    value_block,
    key_segs,
    key_first,
    slot_idx,
):
    running_max, totals, accumulated = carried
    row_count = query_stretch.shape[0]
    score_scale = 1.0 / math.sqrt(query_stretch.shape[-1])
    scores = (
        jnp.einsum("cngd,jnd->ncgj", query_stretch, key_block, preferred_element_type=jnp.float32)
        * score_scale
    )
    query_pos = query_first + jnp.arange(row_count, dtype=jnp.int32)
    key_pos = key_first + jnp.arange(key_block.shape[0], dtype=jnp.int32)
    visible = (key_pos[None, :] <= query_pos[:, None]) & (key_segs[None, :] == query_segs[:, None])
    visible_mask = visible[None, :, None, :]
    scores = jnp.where(visible_mask, scores, masked_score)
    old_max = running_max[slot_idx]
    new_max = jnp.maximum(old_max, jnp.max(scores, axis=-1))
    weights = jnp.where(visible_mask, jnp.exp(scores - new_max[..., None]), 0.0)
    factor = jnp.exp(old_max - new_max)
    new_total = totals[slot_idx] * factor + jnp.sum(weights, axis=-1)
    product = jnp.einsum(
        "ncgj,jnd->ncgd",
        weights.astype(jnp.bfloat16),
        value_block,
        preferred_element_type=jnp.float32,
    )
    new_accum = accumulated[slot_idx] * factor[..., None] + product
    return (
        running_max.at[slot_idx].set(new_max),
        totals.at[slot_idx].set(new_total),
        accumulated.at[slot_idx].set(new_accum),
    )


def make_fold(query_slots, query_segs, query_firsts, segment_ids, half_len):
    stretch_rows = query_slots.shape[1]
    kv_local = query_slots.shape[2]
    head_dim = query_slots.shape[4]

    def fold_keys(carried, piece, start):
        key_piece, value_piece = piece
        piece_rows = key_piece.shape[1]
        block_rows = math.gcd(piece_rows, 512)

        def block_step(block_idx, carried):
            offset = block_idx * block_rows
            for half_idx in range(2):
                key_first = half_idx * half_len + start + offset
                key_block = lax.dynamic_slice_in_dim(
                    key_piece[half_idx], offset, block_rows, 0
                ).reshape(block_rows, kv_local, head_dim)
                value_block = lax.dynamic_slice_in_dim(
                    value_piece[half_idx], offset, block_rows, 0
                ).reshape(block_rows, kv_local, head_dim)
                key_segs = lax.dynamic_slice_in_dim(segment_ids, key_first, block_rows, 0)
                for slot_idx in range(2):
                    needed = key_first <= query_firsts[slot_idx] + stretch_rows - 1
                    update = partial(
                        attend_block,
                        query_stretch=query_slots[slot_idx],
                        query_segs=query_segs[slot_idx],
                        query_first=query_firsts[slot_idx],
                        key_block=key_block,
                        value_block=value_block,
                        key_segs=key_segs,
                        key_first=key_first,
                        slot_idx=slot_idx,
                    )
                    carried = lax.cond(needed, update, keep_state, carried)
            return carried

        return lax.fori_loop(0, piece_rows // block_rows, block_step, carried)

    return fold_keys


def body(queries, key_states, value_states, segment_ids):
    ctx_count = lax.axis_size("ctx")
    ctx_rank = lax.axis_index("ctx")
    bit_count = ctx_count.bit_length() - 1
    stretch_rows = queries.shape[1]
    half_len = stretch_rows * ctx_count
    head_dim = DH
    kv_width = key_states.shape[2]
    kv_local = kv_width // head_dim
    groups = queries.shape[2] // kv_width
    query_firsts = (ctx_rank * stretch_rows, half_len + ctx_rank * stretch_rows)
    query_slots = queries.reshape(2, stretch_rows, kv_local, groups, head_dim)
    query_segs = tuple(
        (
            lax.dynamic_slice_in_dim(segment_ids, query_firsts[slot_idx], stretch_rows, 0)
            for slot_idx in range(2)
        )
    )
    fold_keys = make_fold(query_slots, query_segs, query_firsts, segment_ids, half_len)
    initial = (
        jnp.full((2, kv_local, stretch_rows, groups), masked_score, jnp.float32),
        jnp.zeros((2, kv_local, stretch_rows, groups), jnp.float32),
        jnp.zeros((2, kv_local, stretch_rows, groups, head_dim), jnp.float32),
    )
    carried = fold_keys(
        initial,
        (
            lax.all_gather(key_states, "ctx", axis=1, tiled=True),
            lax.all_gather(value_states, "ctx", axis=1, tiled=True),
        ),
        jnp.int32(0),
    )
    paired = jnp.concatenate([key_states, value_states], axis=2)
    slot_low = paired[0]
    slot_high = paired[1]
    for bit_pos in reversed(range(bit_count)):
        upper_half = ctx_rank // 2**bit_pos % 2 == 1
        outgoing = jnp.where(upper_half, slot_low, slot_high)
        incoming = partner(outgoing, "ctx", bit_pos)
        slot_low = jnp.where(upper_half, incoming, slot_low)
        slot_high = jnp.where(upper_half, slot_high, incoming)
    pages = jnp.concatenate([slot_low, slot_high], axis=0)
    key_pages = pages[:, :kv_width]
    value_pages = pages[:, kv_width:]
    running_max, totals, accumulated = carried
    result = accumulated / totals[..., None]
    result = (
        result.transpose(0, 2, 1, 3, 4)
        .reshape(2, stretch_rows, queries.shape[2])
        .astype(jnp.bfloat16)
    )
    key_cache, value_cache = (
        lax.all_to_all(key_pages, "head", split_axis=0, concat_axis=1, tiled=True),
        lax.all_to_all(value_pages, "head", split_axis=0, concat_axis=1, tiled=True),
    )
    return (result, key_cache, value_cache)


def solution(mesh):
    in_specs = (P(None, "ctx", "head"), P(None, "ctx", "head"), P(None, "ctx", "head"), P())
    out_specs = (P(None, "ctx", "head"), P(("ctx", "head"), None), P(("ctx", "head"), None))
    return jax.shard_map(body, mesh=mesh, in_specs=in_specs, out_specs=out_specs, check_vma=False)
```

profile of v0, /device:TPU:205, one launch (start us, length us, event | category | flops | bytes accessed | tf_op | source)
XLA Modules:
  0.0 363.2 jit_solution(17478953619170599460)
XLA Ops:
  10.8 3.3 collective-permute-done
  14.5 8.1 %collective-permute-done.1 = bf16[192,256]{1,0:T(8,128)(2,1)S(1)} collective-permute-done((bf16[192,256]{1,0:T(8,128)(2,1)S(1)}, bf16[192,256]{1,0:T(8,128)(2,1)S(1)}, u32[]{:S(2)}, u32[]{:S(2)}) %collective-permute-start.1) | collective-permute-done | bytes 98336 | tf_op jit(solution)/shard_map/ppermute | solution.py:16
  23.2 4.2 %collective-permute-done.2 = bf16[192,256]{1,0:T(8,128)(2,1)S(1)} collective-permute-done((bf16[192,256]{1,0:T(8,128)(2,1)S(1)}, bf16[192,256]{1,0:T(8,128)(2,1)S(1)}, u32[]{:S(2)}, u32[]{:S(2)}) %collective-permute-start.2) | collective-permute-done | bytes 98336 | tf_op jit(solution)/shard_map/ppermute | solution.py:16
  28.4 3.5 collective-permute-done.3
  31.9 6.0 %collective-permute-start.4 = (bf16[192,256]{1,0:T(8,128)(2,1)S(1)}, bf16[192,256]{1,0:T(8,128)(2,1)S(1)}, u32[]{:S(2)}, u32[]{:S(2)}) collective-permute-start(bf16[192,256]{1,0:T(8,128)(2,1)S(1)} %broadcast_select_fusion.14), channel_id=1, source_target_pairs={{0,8},{8,0},{16,24},{24,16},{32,40},{40,32},{48,56},{56,48},{64,72... | collective-permute-start | bytes 294920 | tf_op jit(solution)/shard_map/ppermute | solution.py:16
  39.7 5.5 %all-to-all-start = ((bf16[8,48,128]{2,1,0:T(8,128)(2,1)}), bf16[8,48,128]{2,1,0:T(8,128)(2,1)S(1)}, u32[]{:S(2)}, u32[]{:S(2)}) async-start(bf16[8,48,128]{2,1,0:T(8,128)(2,1)} %bitcast.49), calls=%async_computation | async-start | bytes 196608 | tf_op jit(solution)/shard_map/all_to_all | solution.py:159
  46.0 4.4 %all-to-all-done = bf16[8,48,128]{2,1,0:T(8,128)(2,1)S(1)} async-done(((bf16[8,48,128]{2,1,0:T(8,128)(2,1)}), bf16[8,48,128]{2,1,0:T(8,128)(2,1)S(1)}, u32[]{:S(2)}, u32[]{:S(2)}) %all-to-all-start) | async-done | bytes 98336 | tf_op jit(solution)/shard_map/all_to_all | solution.py:159
  50.3 4.8 %all-to-all-start.1 = ((bf16[8,48,128]{2,1,0:T(8,128)(2,1)}), bf16[8,48,128]{2,1,0:T(8,128)(2,1)S(1)}, u32[]{:S(2)}, u32[]{:S(2)}) async-start(bf16[8,48,128]{2,1,0:T(8,128)(2,1)} %bitcast.51), calls=%async_computation.1 | async-start | bytes 196608 | tf_op jit(solution)/shard_map/all_to_all | solution.py:160
  55.8 4.2 %all-to-all-done.1 = bf16[8,48,128]{2,1,0:T(8,128)(2,1)S(1)} async-done(((bf16[8,48,128]{2,1,0:T(8,128)(2,1)}), bf16[8,48,128]{2,1,0:T(8,128)(2,1)S(1)}, u32[]{:S(2)}, u32[]{:S(2)}) %all-to-all-start.1) | async-done | bytes 98336 | tf_op jit(solution)/shard_map/all_to_all | solution.py:160
  60.7 14.2 %all-gather.3.cloned.1.call-done = bf16[2,6144,128]{2,1,0:T(8,128)(2,1)} async-done(((bf16[2,192,128]{2,1,0:T(8,128)(2,1)}), bf16[2,6144,128]{2,1,0:T(8,128)(2,1)}) %all-gather.3.cloned.1.call-update) | async-done | bytes 3145744 | tf_op jit(solution)/shard_map/all_gather | solution.py:134
  74.8 67.7 %all-gather.5.cloned.1.call-done = bf16[2,6144,128]{2,1,0:T(8,128)(2,1)} async-done(((bf16[2,192,128]{2,1,0:T(8,128)(2,1)}), bf16[2,6144,128]{2,1,0:T(8,128)(2,1)}) %all-gather.5.cloned.1.call-update) | async-done | bytes 3145744 | tf_op jit(solution)/shard_map/all_gather | solution.py:135
  142.7 212.0 %while.32 = (s32[]{:T(128)}, f32[2,1,192,8]{3,2,1,0:T(8,128)S(1)}, f32[2,1,192,8]{3,2,1,0:T(8,128)S(1)}, f32[2,1,192,8,128]{4,3,2,1,0:T(8,128)S(1)}, s32[]{:T(12...) while((s32[]{:T(128)}, f32[2,1,192,8]{3,2,1,0:T(8,128)S(1)}, ...), condition=%wide.region_17.18_spmd, body=%wide.region_0.17_spmd.sunk | while | flops 1654287104 | bytes 73090920 | solution.py:102
  144.9 3.3 fusion.110
  148.3 4.1 %conditional.8 = ((f32[2,1,192,8]{3,2,1,0:T(8,128)S(1)}, f32[2,1,192,8]{3,2,1,0:T(8,128)S(1)}, f32[2,1,192,8,128]{4,3,2,1,0:T(8,128)S(1)})) conditional(s32[]{:T(128)} %convert_element_type.108, (f32[2,1,192,8]{3,2,1,0:T(8,128)S(1)}, f32[2,1,192,8]{3,2,1,0:T(8,128)S(1)}, f32[2,1,192,8,128]{4,3,2,1,0:T(8,128)S(1)}) %tuple.152, ...), branch_computations={%region_1.0_spmd, %region_2.4_spmd} | conditional | flops 413571776 | bytes 14469416 | solution.py:99
  152.3 4.1 %conditional.9 = ((f32[2,1,192,8]{3,2,1,0:T(8,128)S(1)}, f32[2,1,192,8]{3,2,1,0:T(8,128)S(1)}, f32[2,1,192,8,128]{4,3,2,1,0:T(8,128)S(1)})) conditional(s32[]{:T(128)} %convert_element_type.107, (f32[2,1,192,8]{3,2,1,0:T(8,128)S(1)}, f32[2,1,192,8]{3,2,1,0:T(8,128)S(1)}, f32[2,1,192,8,128]{4,3,2,1,0:T(8,128)S(1)}) %get-tuple-element.948, ...), branch_computations={%region_5.0_spmd, %region_6.8_spmd} | conditional | flops 413571776 | bytes 14469416 | solution.py:99
  156.5 4.1 %conditional.11 = ((f32[2,1,192,8]{3,2,1,0:T(8,128)S(1)}, f32[2,1,192,8]{3,2,1,0:T(8,128)S(1)}, f32[2,1,192,8,128]{4,3,2,1,0:T(8,128)S(1)})) conditional(s32[]{:T(128)} %convert_element_type.105, (f32[2,1,192,8]{3,2,1,0:T(8,128)S(1)}, f32[2,1,192,8]{3,2,1,0:T(8,128)S(1)}, f32[2,1,192,8,128]{4,3,2,1,0:T(8,128)S(1)}) %get-tuple-element.950, ...), branch_computations={%region_13.0_spmd, %region_14.16_spmd} | conditional | flops 413571776 | bytes 14469416 | solution.py:99
  157.6 1.4 fusion.87
  162.5 3.3 fusion.110
  165.9 4.1 %conditional.8 = ((f32[2,1,192,8]{3,2,1,0:T(8,128)S(1)}, f32[2,1,192,8]{3,2,1,0:T(8,128)S(1)}, f32[2,1,192,8,128]{4,3,2,1,0:T(8,128)S(1)})) conditional(s32[]{:T(128)} %convert_element_type.108, (f32[2,1,192,8]{3,2,1,0:T(8,128)S(1)}, f32[2,1,192,8]{3,2,1,0:T(8,128)S(1)}, f32[2,1,192,8,128]{4,3,2,1,0:T(8,128)S(1)}) %tuple.152, ...), branch_computations={%region_1.0_spmd, %region_2.4_spmd} | conditional | flops 413571776 | bytes 14469416 | solution.py:99
  170.0 4.1 %conditional.9 = ((f32[2,1,192,8]{3,2,1,0:T(8,128)S(1)}, f32[2,1,192,8]{3,2,1,0:T(8,128)S(1)}, f32[2,1,192,8,128]{4,3,2,1,0:T(8,128)S(1)})) conditional(s32[]{:T(128)} %convert_element_type.107, (f32[2,1,192,8]{3,2,1,0:T(8,128)S(1)}, f32[2,1,192,8]{3,2,1,0:T(8,128)S(1)}, f32[2,1,192,8,128]{4,3,2,1,0:T(8,128)S(1)}) %get-tuple-element.948, ...), branch_computations={%region_5.0_spmd, %region_6.8_spmd} | conditional | flops 413571776 | bytes 14469416 | solution.py:99
  174.1 4.1 %conditional.11 = ((f32[2,1,192,8]{3,2,1,0:T(8,128)S(1)}, f32[2,1,192,8]{3,2,1,0:T(8,128)S(1)}, f32[2,1,192,8,128]{4,3,2,1,0:T(8,128)S(1)})) conditional(s32[]{:T(128)} %convert_element_type.105, (f32[2,1,192,8]{3,2,1,0:T(8,128)S(1)}, f32[2,1,192,8]{3,2,1,0:T(8,128)S(1)}, f32[2,1,192,8,128]{4,3,2,1,0:T(8,128)S(1)}) %get-tuple-element.950, ...), branch_computations={%region_13.0_spmd, %region_14.16_spmd} | conditional | flops 413571776 | bytes 14469416 | solution.py:99
  180.2 3.3 fusion.110
  183.6 4.1 %conditional.8 = ((f32[2,1,192,8]{3,2,1,0:T(8,128)S(1)}, f32[2,1,192,8]{3,2,1,0:T(8,128)S(1)}, f32[2,1,192,8,128]{4,3,2,1,0:T(8,128)S(1)})) conditional(s32[]{:T(128)} %convert_element_type.108, (f32[2,1,192,8]{3,2,1,0:T(8,128)S(1)}, f32[2,1,192,8]{3,2,1,0:T(8,128)S(1)}, f32[2,1,192,8,128]{4,3,2,1,0:T(8,128)S(1)}) %tuple.152, ...), branch_computations={%region_1.0_spmd, %region_2.4_spmd} | conditional | flops 413571776 | bytes 14469416 | solution.py:99
  187.6 4.1 %conditional.9 = ((f32[2,1,192,8]{3,2,1,0:T(8,128)S(1)}, f32[2,1,192,8]{3,2,1,0:T(8,128)S(1)}, f32[2,1,192,8,128]{4,3,2,1,0:T(8,128)S(1)})) conditional(s32[]{:T(128)} %convert_element_type.107, (f32[2,1,192,8]{3,2,1,0:T(8,128)S(1)}, f32[2,1,192,8]{3,2,1,0:T(8,128)S(1)}, f32[2,1,192,8,128]{4,3,2,1,0:T(8,128)S(1)}) %get-tuple-element.948, ...), branch_computations={%region_5.0_spmd, %region_6.8_spmd} | conditional | flops 413571776 | bytes 14469416 | solution.py:99
  188.8 1.4 fusion.37
  191.8 4.1 %conditional.11 = ((f32[2,1,192,8]{3,2,1,0:T(8,128)S(1)}, f32[2,1,192,8]{3,2,1,0:T(8,128)S(1)}, f32[2,1,192,8,128]{4,3,2,1,0:T(8,128)S(1)})) conditional(s32[]{:T(128)} %convert_element_type.105, (f32[2,1,192,8]{3,2,1,0:T(8,128)S(1)}, f32[2,1,192,8]{3,2,1,0:T(8,128)S(1)}, f32[2,1,192,8,128]{4,3,2,1,0:T(8,128)S(1)}) %get-tuple-element.950, ...), branch_computations={%region_13.0_spmd, %region_14.16_spmd} | conditional | flops 413571776 | bytes 14469416 | solution.py:99
  197.8 3.3 fusion.110
  201.2 4.1 %conditional.8 = ((f32[2,1,192,8]{3,2,1,0:T(8,128)S(1)}, f32[2,1,192,8]{3,2,1,0:T(8,128)S(1)}, f32[2,1,192,8,128]{4,3,2,1,0:T(8,128)S(1)})) conditional(s32[]{:T(128)} %convert_element_type.108, (f32[2,1,192,8]{3,2,1,0:T(8,128)S(1)}, f32[2,1,192,8]{3,2,1,0:T(8,128)S(1)}, f32[2,1,192,8,128]{4,3,2,1,0:T(8,128)S(1)}) %tuple.152, ...), branch_computations={%region_1.0_spmd, %region_2.4_spmd} | conditional | flops 413571776 | bytes 14469416 | solution.py:99
  205.3 4.1 %conditional.9 = ((f32[2,1,192,8]{3,2,1,0:T(8,128)S(1)}, f32[2,1,192,8]{3,2,1,0:T(8,128)S(1)}, f32[2,1,192,8,128]{4,3,2,1,0:T(8,128)S(1)})) conditional(s32[]{:T(128)} %convert_element_type.107, (f32[2,1,192,8]{3,2,1,0:T(8,128)S(1)}, f32[2,1,192,8]{3,2,1,0:T(8,128)S(1)}, f32[2,1,192,8,128]{4,3,2,1,0:T(8,128)S(1)}) %get-tuple-element.948, ...), branch_computations={%region_5.0_spmd, %region_6.8_spmd} | conditional | flops 413571776 | bytes 14469416 | solution.py:99
  209.4 4.1 %conditional.11 = ((f32[2,1,192,8]{3,2,1,0:T(8,128)S(1)}, f32[2,1,192,8]{3,2,1,0:T(8,128)S(1)}, f32[2,1,192,8,128]{4,3,2,1,0:T(8,128)S(1)})) conditional(s32[]{:T(128)} %convert_element_type.105, (f32[2,1,192,8]{3,2,1,0:T(8,128)S(1)}, f32[2,1,192,8]{3,2,1,0:T(8,128)S(1)}, f32[2,1,192,8,128]{4,3,2,1,0:T(8,128)S(1)}) %get-tuple-element.950, ...), branch_computations={%region_13.0_spmd, %region_14.16_spmd} | conditional | flops 413571776 | bytes 14469416 | solution.py:99
  210.6 1.4 fusion.87
  215.5 3.3 fusion.110
  218.9 4.1 %conditional.8 = ((f32[2,1,192,8]{3,2,1,0:T(8,128)S(1)}, f32[2,1,192,8]{3,2,1,0:T(8,128)S(1)}, f32[2,1,192,8,128]{4,3,2,1,0:T(8,128)S(1)})) conditional(s32[]{:T(128)} %convert_element_type.108, (f32[2,1,192,8]{3,2,1,0:T(8,128)S(1)}, f32[2,1,192,8]{3,2,1,0:T(8,128)S(1)}, f32[2,1,192,8,128]{4,3,2,1,0:T(8,128)S(1)}) %tuple.152, ...), branch_computations={%region_1.0_spmd, %region_2.4_spmd} | conditional | flops 413571776 | bytes 14469416 | solution.py:99
  222.9 4.1 %conditional.9 = ((f32[2,1,192,8]{3,2,1,0:T(8,128)S(1)}, f32[2,1,192,8]{3,2,1,0:T(8,128)S(1)}, f32[2,1,192,8,128]{4,3,2,1,0:T(8,128)S(1)})) conditional(s32[]{:T(128)} %convert_element_type.107, (f32[2,1,192,8]{3,2,1,0:T(8,128)S(1)}, f32[2,1,192,8]{3,2,1,0:T(8,128)S(1)}, f32[2,1,192,8,128]{4,3,2,1,0:T(8,128)S(1)}) %get-tuple-element.948, ...), branch_computations={%region_5.0_spmd, %region_6.8_spmd} | conditional | flops 413571776 | bytes 14469416 | solution.py:99
  227.1 4.1 %conditional.11 = ((f32[2,1,192,8]{3,2,1,0:T(8,128)S(1)}, f32[2,1,192,8]{3,2,1,0:T(8,128)S(1)}, f32[2,1,192,8,128]{4,3,2,1,0:T(8,128)S(1)})) conditional(s32[]{:T(128)} %convert_element_type.105, (f32[2,1,192,8]{3,2,1,0:T(8,128)S(1)}, f32[2,1,192,8]{3,2,1,0:T(8,128)S(1)}, f32[2,1,192,8,128]{4,3,2,1,0:T(8,128)S(1)}) %get-tuple-element.950, ...), branch_computations={%region_13.0_spmd, %region_14.16_spmd} | conditional | flops 413571776 | bytes 14469416 | solution.py:99
  233.1 3.3 fusion.110
  236.5 4.1 %conditional.8 = ((f32[2,1,192,8]{3,2,1,0:T(8,128)S(1)}, f32[2,1,192,8]{3,2,1,0:T(8,128)S(1)}, f32[2,1,192,8,128]{4,3,2,1,0:T(8,128)S(1)})) conditional(s32[]{:T(128)} %convert_element_type.108, (f32[2,1,192,8]{3,2,1,0:T(8,128)S(1)}, f32[2,1,192,8]{3,2,1,0:T(8,128)S(1)}, f32[2,1,192,8,128]{4,3,2,1,0:T(8,128)S(1)}) %tuple.152, ...), branch_computations={%region_1.0_spmd, %region_2.4_spmd} | conditional | flops 413571776 | bytes 14469416 | solution.py:99
  240.6 4.1 %conditional.9 = ((f32[2,1,192,8]{3,2,1,0:T(8,128)S(1)}, f32[2,1,192,8]{3,2,1,0:T(8,128)S(1)}, f32[2,1,192,8,128]{4,3,2,1,0:T(8,128)S(1)})) conditional(s32[]{:T(128)} %convert_element_type.107, (f32[2,1,192,8]{3,2,1,0:T(8,128)S(1)}, f32[2,1,192,8]{3,2,1,0:T(8,128)S(1)}, f32[2,1,192,8,128]{4,3,2,1,0:T(8,128)S(1)}) %get-tuple-element.948, ...), branch_computations={%region_5.0_spmd, %region_6.8_spmd} | conditional | flops 413571776 | bytes 14469416 | solution.py:99
  244.7 4.1 %conditional.11 = ((f32[2,1,192,8]{3,2,1,0:T(8,128)S(1)}, f32[2,1,192,8]{3,2,1,0:T(8,128)S(1)}, f32[2,1,192,8,128]{4,3,2,1,0:T(8,128)S(1)})) conditional(s32[]{:T(128)} %convert_element_type.105, (f32[2,1,192,8]{3,2,1,0:T(8,128)S(1)}, f32[2,1,192,8]{3,2,1,0:T(8,128)S(1)}, f32[2,1,192,8,128]{4,3,2,1,0:T(8,128)S(1)}) %get-tuple-element.950, ...), branch_computations={%region_13.0_spmd, %region_14.16_spmd} | conditional | flops 413571776 | bytes 14469416 | solution.py:99
  250.8 3.3 fusion.110
  254.2 4.1 %conditional.8 = ((f32[2,1,192,8]{3,2,1,0:T(8,128)S(1)}, f32[2,1,192,8]{3,2,1,0:T(8,128)S(1)}, f32[2,1,192,8,128]{4,3,2,1,0:T(8,128)S(1)})) conditional(s32[]{:T(128)} %convert_element_type.108, (f32[2,1,192,8]{3,2,1,0:T(8,128)S(1)}, f32[2,1,192,8]{3,2,1,0:T(8,128)S(1)}, f32[2,1,192,8,128]{4,3,2,1,0:T(8,128)S(1)}) %tuple.152, ...), branch_computations={%region_1.0_spmd, %region_2.4_spmd} | conditional | flops 413571776 | bytes 14469416 | solution.py:99
  258.2 4.1 %conditional.9 = ((f32[2,1,192,8]{3,2,1,0:T(8,128)S(1)}, f32[2,1,192,8]{3,2,1,0:T(8,128)S(1)}, f32[2,1,192,8,128]{4,3,2,1,0:T(8,128)S(1)})) conditional(s32[]{:T(128)} %convert_element_type.107, (f32[2,1,192,8]{3,2,1,0:T(8,128)S(1)}, f32[2,1,192,8]{3,2,1,0:T(8,128)S(1)}, f32[2,1,192,8,128]{4,3,2,1,0:T(8,128)S(1)}) %get-tuple-element.948, ...), branch_computations={%region_5.0_spmd, %region_6.8_spmd} | conditional | flops 413571776 | bytes 14469416 | solution.py:99
  262.4 4.1 %conditional.11 = ((f32[2,1,192,8]{3,2,1,0:T(8,128)S(1)}, f32[2,1,192,8]{3,2,1,0:T(8,128)S(1)}, f32[2,1,192,8,128]{4,3,2,1,0:T(8,128)S(1)})) conditional(s32[]{:T(128)} %convert_element_type.105, (f32[2,1,192,8]{3,2,1,0:T(8,128)S(1)}, f32[2,1,192,8]{3,2,1,0:T(8,128)S(1)}, f32[2,1,192,8,128]{4,3,2,1,0:T(8,128)S(1)}) %get-tuple-element.950, ...), branch_computations={%region_13.0_spmd, %region_14.16_spmd} | conditional | flops 413571776 | bytes 14469416 | solution.py:99
  268.4 3.3 fusion.110
  271.8 4.1 %conditional.8 = ((f32[2,1,192,8]{3,2,1,0:T(8,128)S(1)}, f32[2,1,192,8]{3,2,1,0:T(8,128)S(1)}, f32[2,1,192,8,128]{4,3,2,1,0:T(8,128)S(1)})) conditional(s32[]{:T(128)} %convert_element_type.108, (f32[2,1,192,8]{3,2,1,0:T(8,128)S(1)}, f32[2,1,192,8]{3,2,1,0:T(8,128)S(1)}, f32[2,1,192,8,128]{4,3,2,1,0:T(8,128)S(1)}) %tuple.152, ...), branch_computations={%region_1.0_spmd, %region_2.4_spmd} | conditional | flops 413571776 | bytes 14469416 | solution.py:99
  275.9 4.1 %conditional.9 = ((f32[2,1,192,8]{3,2,1,0:T(8,128)S(1)}, f32[2,1,192,8]{3,2,1,0:T(8,128)S(1)}, f32[2,1,192,8,128]{4,3,2,1,0:T(8,128)S(1)})) conditional(s32[]{:T(128)} %convert_element_type.107, (f32[2,1,192,8]{3,2,1,0:T(8,128)S(1)}, f32[2,1,192,8]{3,2,1,0:T(8,128)S(1)}, f32[2,1,192,8,128]{4,3,2,1,0:T(8,128)S(1)}) %get-tuple-element.948, ...), branch_computations={%region_5.0_spmd, %region_6.8_spmd} | conditional | flops 413571776 | bytes 14469416 | solution.py:99
  280.0 4.1 %conditional.11 = ((f32[2,1,192,8]{3,2,1,0:T(8,128)S(1)}, f32[2,1,192,8]{3,2,1,0:T(8,128)S(1)}, f32[2,1,192,8,128]{4,3,2,1,0:T(8,128)S(1)})) conditional(s32[]{:T(128)} %convert_element_type.105, (f32[2,1,192,8]{3,2,1,0:T(8,128)S(1)}, f32[2,1,192,8]{3,2,1,0:T(8,128)S(1)}, f32[2,1,192,8,128]{4,3,2,1,0:T(8,128)S(1)}) %get-tuple-element.950, ...), branch_computations={%region_13.0_spmd, %region_14.16_spmd} | conditional | flops 413571776 | bytes 14469416 | solution.py:99
  286.1 3.3 fusion.110
  289.5 4.1 %conditional.8 = ((f32[2,1,192,8]{3,2,1,0:T(8,128)S(1)}, f32[2,1,192,8]{3,2,1,0:T(8,128)S(1)}, f32[2,1,192,8,128]{4,3,2,1,0:T(8,128)S(1)})) conditional(s32[]{:T(128)} %convert_element_type.108, (f32[2,1,192,8]{3,2,1,0:T(8,128)S(1)}, f32[2,1,192,8]{3,2,1,0:T(8,128)S(1)}, f32[2,1,192,8,128]{4,3,2,1,0:T(8,128)S(1)}) %tuple.152, ...), branch_computations={%region_1.0_spmd, %region_2.4_spmd} | conditional | flops 413571776 | bytes 14469416 | solution.py:99
  293.5 4.1 %conditional.9 = ((f32[2,1,192,8]{3,2,1,0:T(8,128)S(1)}, f32[2,1,192,8]{3,2,1,0:T(8,128)S(1)}, f32[2,1,192,8,128]{4,3,2,1,0:T(8,128)S(1)})) conditional(s32[]{:T(128)} %convert_element_type.107, (f32[2,1,192,8]{3,2,1,0:T(8,128)S(1)}, f32[2,1,192,8]{3,2,1,0:T(8,128)S(1)}, f32[2,1,192,8,128]{4,3,2,1,0:T(8,128)S(1)}) %get-tuple-element.948, ...), branch_computations={%region_5.0_spmd, %region_6.8_spmd} | conditional | flops 413571776 | bytes 14469416 | solution.py:99
  294.7 1.4 fusion.37
  297.7 4.1 %conditional.11 = ((f32[2,1,192,8]{3,2,1,0:T(8,128)S(1)}, f32[2,1,192,8]{3,2,1,0:T(8,128)S(1)}, f32[2,1,192,8,128]{4,3,2,1,0:T(8,128)S(1)})) conditional(s32[]{:T(128)} %convert_element_type.105, (f32[2,1,192,8]{3,2,1,0:T(8,128)S(1)}, f32[2,1,192,8]{3,2,1,0:T(8,128)S(1)}, f32[2,1,192,8,128]{4,3,2,1,0:T(8,128)S(1)}) %get-tuple-element.950, ...), branch_computations={%region_13.0_spmd, %region_14.16_spmd} | conditional | flops 413571776 | bytes 14469416 | solution.py:99
  303.7 3.3 fusion.110
  307.1 4.1 %conditional.8 = ((f32[2,1,192,8]{3,2,1,0:T(8,128)S(1)}, f32[2,1,192,8]{3,2,1,0:T(8,128)S(1)}, f32[2,1,192,8,128]{4,3,2,1,0:T(8,128)S(1)})) conditional(s32[]{:T(128)} %convert_element_type.108, (f32[2,1,192,8]{3,2,1,0:T(8,128)S(1)}, f32[2,1,192,8]{3,2,1,0:T(8,128)S(1)}, f32[2,1,192,8,128]{4,3,2,1,0:T(8,128)S(1)}) %tuple.152, ...), branch_computations={%region_1.0_spmd, %region_2.4_spmd} | conditional | flops 413571776 | bytes 14469416 | solution.py:99
  311.2 4.1 %conditional.9 = ((f32[2,1,192,8]{3,2,1,0:T(8,128)S(1)}, f32[2,1,192,8]{3,2,1,0:T(8,128)S(1)}, f32[2,1,192,8,128]{4,3,2,1,0:T(8,128)S(1)})) conditional(s32[]{:T(128)} %convert_element_type.107, (f32[2,1,192,8]{3,2,1,0:T(8,128)S(1)}, f32[2,1,192,8]{3,2,1,0:T(8,128)S(1)}, f32[2,1,192,8,128]{4,3,2,1,0:T(8,128)S(1)}) %get-tuple-element.948, ...), branch_computations={%region_5.0_spmd, %region_6.8_spmd} | conditional | flops 413571776 | bytes 14469416 | solution.py:99
  315.3 4.1 %conditional.11 = ((f32[2,1,192,8]{3,2,1,0:T(8,128)S(1)}, f32[2,1,192,8]{3,2,1,0:T(8,128)S(1)}, f32[2,1,192,8,128]{4,3,2,1,0:T(8,128)S(1)})) conditional(s32[]{:T(128)} %convert_element_type.105, (f32[2,1,192,8]{3,2,1,0:T(8,128)S(1)}, f32[2,1,192,8]{3,2,1,0:T(8,128)S(1)}, f32[2,1,192,8,128]{4,3,2,1,0:T(8,128)S(1)}) %get-tuple-element.950, ...), branch_computations={%region_13.0_spmd, %region_14.16_spmd} | conditional | flops 413571776 | bytes 14469416 | solution.py:99
  321.4 3.3 fusion.110
  324.8 4.1 %conditional.8 = ((f32[2,1,192,8]{3,2,1,0:T(8,128)S(1)}, f32[2,1,192,8]{3,2,1,0:T(8,128)S(1)}, f32[2,1,192,8,128]{4,3,2,1,0:T(8,128)S(1)})) conditional(s32[]{:T(128)} %convert_element_type.108, (f32[2,1,192,8]{3,2,1,0:T(8,128)S(1)}, f32[2,1,192,8]{3,2,1,0:T(8,128)S(1)}, f32[2,1,192,8,128]{4,3,2,1,0:T(8,128)S(1)}) %tuple.152, ...), branch_computations={%region_1.0_spmd, %region_2.4_spmd} | conditional | flops 413571776 | bytes 14469416 | solution.py:99
  328.8 4.1 %conditional.9 = ((f32[2,1,192,8]{3,2,1,0:T(8,128)S(1)}, f32[2,1,192,8]{3,2,1,0:T(8,128)S(1)}, f32[2,1,192,8,128]{4,3,2,1,0:T(8,128)S(1)})) conditional(s32[]{:T(128)} %convert_element_type.107, (f32[2,1,192,8]{3,2,1,0:T(8,128)S(1)}, f32[2,1,192,8]{3,2,1,0:T(8,128)S(1)}, f32[2,1,192,8,128]{4,3,2,1,0:T(8,128)S(1)}) %get-tuple-element.948, ...), branch_computations={%region_5.0_spmd, %region_6.8_spmd} | conditional | flops 413571776 | bytes 14469416 | solution.py:99
  333.0 4.1 %conditional.11 = ((f32[2,1,192,8]{3,2,1,0:T(8,128)S(1)}, f32[2,1,192,8]{3,2,1,0:T(8,128)S(1)}, f32[2,1,192,8,128]{4,3,2,1,0:T(8,128)S(1)})) conditional(s32[]{:T(128)} %convert_element_type.105, (f32[2,1,192,8]{3,2,1,0:T(8,128)S(1)}, f32[2,1,192,8]{3,2,1,0:T(8,128)S(1)}, f32[2,1,192,8,128]{4,3,2,1,0:T(8,128)S(1)}) %get-tuple-element.950, ...), branch_computations={%region_13.0_spmd, %region_14.16_spmd} | conditional | flops 413571776 | bytes 14469416 | solution.py:99
  339.0 3.3 fusion.110
  342.4 4.1 %conditional.8 = ((f32[2,1,192,8]{3,2,1,0:T(8,128)S(1)}, f32[2,1,192,8]{3,2,1,0:T(8,128)S(1)}, f32[2,1,192,8,128]{4,3,2,1,0:T(8,128)S(1)})) conditional(s32[]{:T(128)} %convert_element_type.108, (f32[2,1,192,8]{3,2,1,0:T(8,128)S(1)}, f32[2,1,192,8]{3,2,1,0:T(8,128)S(1)}, f32[2,1,192,8,128]{4,3,2,1,0:T(8,128)S(1)}) %tuple.152, ...), branch_computations={%region_1.0_spmd, %region_2.4_spmd} | conditional | flops 413571776 | bytes 14469416 | solution.py:99
  346.5 4.1 %conditional.9 = ((f32[2,1,192,8]{3,2,1,0:T(8,128)S(1)}, f32[2,1,192,8]{3,2,1,0:T(8,128)S(1)}, f32[2,1,192,8,128]{4,3,2,1,0:T(8,128)S(1)})) conditional(s32[]{:T(128)} %convert_element_type.107, (f32[2,1,192,8]{3,2,1,0:T(8,128)S(1)}, f32[2,1,192,8]{3,2,1,0:T(8,128)S(1)}, f32[2,1,192,8,128]{4,3,2,1,0:T(8,128)S(1)}) %get-tuple-element.948, ...), branch_computations={%region_5.0_spmd, %region_6.8_spmd} | conditional | flops 413571776 | bytes 14469416 | solution.py:99
  350.6 4.1 %conditional.11 = ((f32[2,1,192,8]{3,2,1,0:T(8,128)S(1)}, f32[2,1,192,8]{3,2,1,0:T(8,128)S(1)}, f32[2,1,192,8,128]{4,3,2,1,0:T(8,128)S(1)})) conditional(s32[]{:T(128)} %convert_element_type.105, (f32[2,1,192,8]{3,2,1,0:T(8,128)S(1)}, f32[2,1,192,8]{3,2,1,0:T(8,128)S(1)}, f32[2,1,192,8,128]{4,3,2,1,0:T(8,128)S(1)}) %get-tuple-element.950, ...), branch_computations={%region_13.0_spmd, %region_14.16_spmd} | conditional | flops 413571776 | bytes 14469416 | solution.py:99
  (433 shorter events, 174.4 us)
Async XLA Ops:
  7.2 30.8 %copy-start = (bf16[2,192,1024]{2,1,0:T(8,128)(2,1)S(1)}, bf16[2,192,1024]{2,1,0:T(8,128)(2,1)}, u32[]{:S(2)}) copy-start(bf16[2,192,1024]{2,1,0:T(8,128)(2,1)} %param.38) | copy-start | bytes 2359300
  7.2 67.7 %all-gather.3.cloned.1.call-start = ((), (), s32[]{:S(2)}) async-start(), calls=%async_computation.2 | async-start | bytes 3244032 | tf_op jit(solution)/shard_map/all_gather | solution.py:134
  7.9 134.6 %all-gather.5.cloned.1.call-start = ((), (), s32[]{:S(2)}) async-start(), calls=%async_computation.3 | async-start | bytes 3244032 | tf_op jit(solution)/shard_map/all_gather | solution.py:135
  10.5 3.6 collective-permute-start
  14.1 8.4 %collective-permute-start.1 = (bf16[192,256]{1,0:T(8,128)(2,1)S(1)}, bf16[192,256]{1,0:T(8,128)(2,1)S(1)}, u32[]{:S(2)}, u32[]{:S(2)}) collective-permute-start(bf16[192,256]{1,0:T(8,128)(2,1)S(1)} %get-tuple-element.704), channel_id=1, source_target_pairs={{0,64},{8,72},{16,80},{24,88},{32,96},{40,104},{48,112},{56,120},{... | collective-permute-start | bytes 294920 | tf_op jit(solution)/shard_map/ppermute | solution.py:16
  22.6 4.8 %collective-permute-start.2 = (bf16[192,256]{1,0:T(8,128)(2,1)S(1)}, bf16[192,256]{1,0:T(8,128)(2,1)S(1)}, u32[]{:S(2)}, u32[]{:S(2)}) collective-permute-start(bf16[192,256]{1,0:T(8,128)(2,1)S(1)} %broadcast_select_fusion.8), channel_id=1, source_target_pairs={{0,32},{8,40},{16,48},{24,56},{32,0},{40,8},{48,16},{56,24},{64,96... | collective-permute-start | bytes 294920 | tf_op jit(solution)/shard_map/ppermute | solution.py:16
  27.4 4.4 %collective-permute-start.3 = (bf16[192,256]{1,0:T(8,128)(2,1)S(1)}, bf16[192,256]{1,0:T(8,128)(2,1)S(1)}, u32[]{:S(2)}, u32[]{:S(2)}) collective-permute-start(bf16[192,256]{1,0:T(8,128)(2,1)S(1)} %get-tuple-element.701), channel_id=1, source_target_pairs={{0,16},{8,24},{16,0},{24,8},{32,48},{40,56},{48,32},{56,40},{64,80... | collective-permute-start | bytes 294920 | tf_op jit(solution)/shard_map/ppermute | solution.py:16
  31.9 7.1 %collective-permute-start.4 = (bf16[192,256]{1,0:T(8,128)(2,1)S(1)}, bf16[192,256]{1,0:T(8,128)(2,1)S(1)}, u32[]{:S(2)}, u32[]{:S(2)}) collective-permute-start(bf16[192,256]{1,0:T(8,128)(2,1)S(1)} %broadcast_select_fusion.14), channel_id=1, source_target_pairs={{0,8},{8,0},{16,24},{24,16},{32,40},{40,32},{48,56},{56,48},{64,72... | collective-permute-start | bytes 294920 | tf_op jit(solution)/shard_map/ppermute | solution.py:16
  39.7 10.6 %all-to-all-start = ((bf16[8,48,128]{2,1,0:T(8,128)(2,1)}), bf16[8,48,128]{2,1,0:T(8,128)(2,1)S(1)}, u32[]{:S(2)}, u32[]{:S(2)}) async-start(bf16[8,48,128]{2,1,0:T(8,128)(2,1)} %bitcast.49), calls=%async_computation | async-start | bytes 196608 | tf_op jit(solution)/shard_map/all_to_all | solution.py:159
  50.3 9.7 %all-to-all-start.1 = ((bf16[8,48,128]{2,1,0:T(8,128)(2,1)}), bf16[8,48,128]{2,1,0:T(8,128)(2,1)S(1)}, u32[]{:S(2)}, u32[]{:S(2)}) async-start(bf16[8,48,128]{2,1,0:T(8,128)(2,1)} %bitcast.51), calls=%async_computation.1 | async-start | bytes 196608 | tf_op jit(solution)/shard_map/all_to_all | solution.py:160
Sparse Core Ops, SparseCore 0:
  9.8 64.9 all-gather.2
  76.6 65.8 all-gather.4
where the time goes:
time: 365 us; the launch traced here: 363 us
  waiting for transfers between devices  111 us (30%)
  matrix products  82.6 us (23%)
  local copies, waits for them, and re-layouts  71.8 us (20%)
  other arithmetic  61.1 us (17%)
  starting transfers between devices  18.6 us (5%)
  between operations  14.2 us (4%)
  loops' own time  4.22 us (1%)
    all_gather x1, waiting for transfers between devices, body(): lax.all_gather(value_states, 'ctx', axis=1, tiled=True)  67.7 us
    dot_general x36, matrix products, attend_block(): jnp.einsum('ncgj,jnd->ncgd', weights.astype(jnp.bfloat16), value_block, p...  50.3 us
    reduce_sum x36, other arithmetic, attend_block(): new_total = totals[slot_idx] * factor + jnp.sum(weights, axis=-1)  49.9 us
    slice x12, local copies, waits for them, and re-layouts, block_step(): value_piece[half_idx]  39.2 us
    dot_general x36, matrix products, attend_block(): jnp.einsum('cngd,jnd->ncgj', query_stretch, key_block, preferred_element_...  32.2 us
    ppermute x5, waiting for transfers between devices, partner(): lax.ppermute(x, axis, [(i, i ^ 1 << distance) for i in range(lax.axis_siz...  19.1 us
    all_gather x1, waiting for transfers between devices, body(): lax.all_gather(key_states, 'ctx', axis=1, tiled=True)  14.2 us
    squeeze x12, local copies, waits for them, and re-layouts, block_step(): query_slots[slot_idx]  14 us
  transfers between devices with their start and end apart: 9, of which 8 were waited for; matrix products, arithmetic and copies ran while one was open for 2% of the time, Pallas kernels for 0%

commit v1 on v0

v1 whole, which is shorter than its diff:
```python
import math

import jax
import jax.numpy as jnp
from jax import lax
from jax.experimental import pallas as pl
from jax.experimental.pallas import tpu as pltpu
from jax.sharding import PartitionSpec as P

MESH = pl.DeviceIdType.MESH
DH = 128
GROUPS = 8
ROWS = 192
CTX = 32
HEAD = 8
KEYS = 4 * ROWS
CACHE = 48
TILE = 2
OTHER = -(2.0 ** 20)
LATER = -(2.0 ** 22)
START = -(2.0 ** 23)
SCALE = math.log2(math.e) / math.sqrt(DH)

LOW, HIGH = 0, 1


def transfers():
    out = {}

    def add(name, link, row, dz, half, source):
        out[name] = (link, row, dz, half, source)

    for half, tag in ((LOW, "L"), (HIGH, "H")):
        for d in (1, 2, 3):
            add(f"U{d}{tag}", "up", 0, -d, half, f"U{d - 1}{tag}" if d > 1 else None)
            add(f"D{d}{tag}", "down", 0, d, half, f"D{d - 1}{tag}" if d > 1 else None)
        add(f"Y0{tag}", "y", 1, 0, half, None)
        for d in (1, 2):
            add(f"YU{d}{tag}", "y", 1, -d, half, f"U{d}{tag}")
            add(f"YD{d}{tag}", "y", 1, d, half, f"D{d}{tag}")
        add(f"OU3{tag}", "up", 1, -3, half, f"YU2{tag}")
        add(f"OD3{tag}", "down", 1, 3, half, f"YD2{tag}")
    add("U4L", "up", 0, -4, LOW, "U3L")
    add("D4H", "down", 0, 4, HIGH, "D3H")
    add("OU4L", "up", 1, -4, LOW, "OU3L")
    add("OD4H", "down", 1, 4, HIGH, "OD3H")
    for name in list(out):
        link, row, dz, half, source = out[name]
        add("C" + name, "core", row, dz, half, name)
    add("C0L", "core", 0, 0, LOW, None)
    add("C0H", "core", 0, 0, HIGH, None)
    return {
        name + tag: (link, row, dz, half, kv, source and source + tag)
        for name, (link, row, dz, half, source) in out.items()
        for kv, tag in ((0, "k"), (1, "v"))
    }


TRANSFERS = transfers()
INDEX = {name: i for i, name in enumerate(TRANSFERS)}
FORWARDS = {name: [k for k, v in TRANSFERS.items() if v[5] == name] for name in TRANSFERS}
FIRST = [n + half + kv for half in "LH" for kv in "kv" for n in ("U1", "D1", "Y0", "C0")]

ARRIVALS = [
    ["U1L", "D1L", "Y0L"],
    ["U1H", "D1H", "Y0H"],
    ["U2L", "D2L", "YU1L"],
    ["U2H", "D2H", "YD1L"],
    ["U3L", "D3L", "YU2L"],
    ["U3H", "D3H", "YD2L"],
    ["U4L", "D4H", "YU2H"],
    ["OU3L", "OD3L", "YD2H"],
    ["OU3H", "OD3H", "YU1H"],
    ["OU4L", "OD4H", "YD1H"],
]
OWN, NEAR, FAR, OPP = 0, 1, 2, 3
PLAN = [
    2,
    (OWN, 0, LOW),
    3,
    (NEAR, 0, LOW),
    (NEAR, 0, HIGH),
    4,
    (OWN, 1, LOW),
    5,
    (FAR, 0, LOW),
    (FAR, 0, HIGH),
    6,
    (NEAR, 1, LOW),
    (OPP, 0, LOW),
    7,
    (OPP, 0, HIGH),
    (FAR, 1, LOW),
    8,
    (FAR, 1, HIGH),
    9,
    (OPP, 1, LOW),
    (OWN, 1, HIGH),
    (NEAR, 1, HIGH),
    (OPP, 1, HIGH),
]


REACH = {OWN: (0, 1), NEAR: (1, 2), FAR: (2, 3), OPP: (3, 4)}


def needs(kind, row, half):
    return [
        name
        for name, (link, r, dz, hf, kv, _) in TRANSFERS.items()
        if link == "core" and r == row and hf == half and abs(dz) in REACH[kind]
    ]


def steps_of(plan):
    jobs, before, pending, seen = [], [], [], set(needs(OWN, 0, LOW) + needs(OWN, 0, HIGH))
    for entry in plan:
        if isinstance(entry, int):
            pending.append(entry)
        else:
            jobs.append(entry)
            fresh = [name for name in needs(*entry) if name not in seen]
            seen.update(fresh)
            before.append((pending, fresh))
            pending = []
    assert seen == {name for name in TRANSFERS if TRANSFERS[name][0] == "core"}
    return jobs, before


JOBS, BEFORE = steps_of(PLAN)


def kernel(q_ref, k_ref, v_ref, seg_ref, out_ref, kc_ref, vc_ref, buf, kfeat, qx, acc, peak, send, recv, csend, crecv):
    c = lax.axis_index("ctx")
    h = lax.axis_index("head")
    y, z, core = c // 16, (c % 16) // 2, c % 2

    def index_of(row, zz, kk):
        return row * 16 + (zz % 8) * 2 + kk

    up_to = index_of(y, z + 1, core)
    down_to = index_of(y, z + 7, core)
    y_to = index_of(1 - y, z, core)
    core_to = index_of(y, z, 1 - core)
    target = {"up": up_to, "down": down_to, "y": y_to, "core": core_to}

    barrier = pltpu.get_barrier_semaphore()
    for peer in (up_to, down_to, y_to, core_to):
        pl.semaphore_signal(barrier, inc=1, device_id=(peer, h), device_id_type=MESH)
    for d in range(1, HEAD):
        pl.semaphore_signal(barrier, inc=1, device_id=(c, (h + d) % HEAD), device_id_type=MESH)

    buf[0, c] = k_ref[0]
    buf[1, c] = v_ref[0]
    buf[2, c] = k_ref[1]
    buf[3, c] = v_ref[1]
    pl.semaphore_wait(barrier, 4 + HEAD - 1)

    def copy_of(name):
        link, row, dz, half, kv, _ = TRANSFERS[name]
        if link == "up":
            block = index_of(y if row == 0 else 1 - y, z + dz + 1 + 8, core)
        elif link == "down":
            block = index_of(y if row == 0 else 1 - y, z + dz - 1 + 8, core)
        elif link == "y":
            block = index_of(y, z + dz + 8, core)
        else:
            block = index_of(y if row == 0 else 1 - y, z + dz + 8, core)
        ref = buf.at[2 * half + kv, block]
        i = INDEX[name]
        return pltpu.make_async_remote_copy(
            src_ref=ref,
            dst_ref=ref,
            send_sem=send.at[i],
            recv_sem=recv.at[i],
            device_id=(target[link], h),
            device_id_type=MESH,
        )

    for name in FIRST:
        copy_of(name).start()

    def arrive(names):
        for name in [n + kv for kv in "kv" for n in names]:
            copy_of(name).wait_recv()
            for onward in FORWARDS[name]:
                copy_of(onward).start()

    seg = seg_ref[...]
    lane = lax.broadcasted_iota(jnp.int32, (1, DH), 1)
    low = jnp.zeros((1, DH), jnp.float32)
    high = jnp.zeros((1, DH), jnp.float32)
    for s in range(4):
        below = jnp.sum(jnp.where(seg < s, 1.0, 0.0), axis=(0, 1), keepdims=True)
        upto = jnp.sum(jnp.where(seg <= s, 1.0, 0.0), axis=(0, 1), keepdims=True)
        low = jnp.where(lane == s, below, low)
        high = jnp.where(lane == s, upto, high)
    used = jnp.where(lane < 4, 1.0, 0.0)

    def inside(first, rows):
        at = (lax.broadcasted_iota(jnp.int32, (rows, DH), 0) + first).astype(jnp.float32)
        return jnp.where((at >= low) & (at < high), 1.0, 0.0)

    def prepare_keys(i, carry):
        kfeat[i] = inside(i * ROWS, ROWS).astype(jnp.bfloat16)
        return carry

    for s in range(2):
        feature = ((used - inside(s * CTX * ROWS + c * ROWS, ROWS)) * OTHER).astype(jnp.bfloat16)
        for g in range(GROUPS):
            qx[s, g, :, :DH] = q_ref[s, :, g * DH : (g + 1) * DH]
            qx[s, g, :, DH:] = feature
    lax.fori_loop(0, 2 * CTX, prepare_keys, 0)
    peak[...] = jnp.full(peak.shape, START, jnp.float32)
    acc[...] = jnp.zeros(acc.shape, jnp.float32)

    rows = TILE * ROWS
    lanes = KEYS // DH
    ones = jnp.ones((KEYS, DH), jnp.bfloat16)

    def attend(qs, half, block, causal):
        first = block * 4
        keys = buf[2 * half, pl.ds(first, 4)].reshape(KEYS, DH)
        values = buf[2 * half + 1, pl.ds(first, 4)].reshape(KEYS, DH)
        features = kfeat[pl.ds(half * CTX + first, 4)].reshape(KEYS, DH)
        keys = jnp.concatenate([keys, features], axis=1)
        values = jnp.concatenate([values, ones], axis=1)
        if causal:
            at = c * ROWS - first * ROWS
            row = lax.broadcasted_iota(jnp.int32, (ROWS, KEYS), 0) + at
            col = lax.broadcasted_iota(jnp.int32, (ROWS, KEYS), 1)
            seen = jnp.concatenate([row >= col] * TILE, axis=0)
        for t in range(GROUPS // TILE):
            heads = pl.ds(t * TILE, TILE)
            queries = qx[qs, heads].reshape(rows, 2 * DH)
            scores = lax.dot_general(
                queries, keys, (((1,), (1,)), ((), ())), preferred_element_type=jnp.float32
            )
            if causal:
                scores = jnp.where(seen, scores, LATER)
            parts = [scores[:, i * DH : (i + 1) * DH] for i in range(lanes)]
            top = parts[0]
            for part in parts[1:]:
                top = jnp.maximum(top, part)
            old = peak[qs, heads].reshape(rows, DH)
            new = jnp.maximum(old, jnp.max(top, axis=1, keepdims=True))
            weights = jnp.concatenate(
                [jnp.exp2((part - new) * SCALE).astype(jnp.bfloat16) for part in parts], axis=1
            )
            factor = jnp.exp2((old - new) * SCALE)
            product = jnp.dot(weights, values, preferred_element_type=jnp.float32)
            held = acc[qs, heads].reshape(rows, 2 * DH)
            held = held * jnp.concatenate([factor, factor], axis=1) + product
            acc[qs, heads] = held.reshape(TILE, ROWS, 2 * DH)
            peak[qs, heads] = new.reshape(TILE, ROWS, DH)

    zb = z // 2
    own = y * 4 + zb
    toward = 1 - 2 * (z % 2)

    arrive(ARRIVALS[0])
    arrive(ARRIVALS[1])
    for name in needs(OWN, 0, LOW) + needs(OWN, 0, HIGH):
        copy_of(name).wait_recv()

    def own_step(half, carry):
        attend(half, half, own, True)
        return carry

    lax.fori_loop(0, 2, own_step, 0)

    def step_body(step, carry):
        def pick(values):
            value = jnp.int32(values[0])
            for i in range(1, len(values)):
                if values[i] != values[0]:
                    value = jnp.where(step == i, jnp.int32(values[i]), value)
            return value

        for i, (events, names) in enumerate(BEFORE):
            if events or names:

                @pl.when(step == i)
                def _(events=events, names=names):
                    for event in events:
                        arrive(ARRIVALS[event])
                    for name in names:
                        copy_of(name).wait_recv()

        row = pick([job[1] for job in JOBS])
        half = pick([job[2] for job in JOBS])
        move = pick([{OWN: 0, NEAR: 0, FAR: 0, OPP: 2}[job[0]] for job in JOBS]) + toward * pick(
            [{OWN: 0, NEAR: -1, FAR: 1, OPP: 0}[job[0]] for job in JOBS]
        )
        block = jnp.where(row == 0, y, 1 - y) * 4 + (zb + move + 4) % 4
        qs = jnp.where(jnp.logical_or(half == 1, block >= own), 1, 0)

        @pl.when(jnp.logical_or(half == 0, block < own))
        def _():
            attend(qs, half, block, False)

        return carry

    lax.fori_loop(0, len(JOBS), step_body, 0)

    half = c // 16

    def cache_source(kv, to):
        return buf.at[2 * half + kv, 2 * (c % 16) + to // 4, pl.ds(pl.multiple_of(CACHE * (to % 4), 16), CACHE)]

    columns = pl.ds(pl.multiple_of(h * DH, DH), DH)

    def cache_copies(d):
        to = (h + d) % HEAD
        return [
            pltpu.make_async_remote_copy(
                src_ref=cache_source(kv, to),
                dst_ref=ref.at[:, columns],
                send_sem=csend.at[kv, d],
                recv_sem=crecv.at[kv, d],
                device_id=(c, to),
                device_id_type=MESH,
            )
            for kv, ref in ((0, kc_ref), (1, vc_ref))
        ]

    for d in range(1, HEAD):
        for copy in cache_copies(d):
            copy.start()
    for kv, ref in ((0, kc_ref), (1, vc_ref)):
        ref[:, columns] = buf[2 * half + kv, 2 * (c % 16) + h // 4, pl.ds(pl.multiple_of(CACHE * (h % 4), 16), CACHE)]

    def finish(g, carry):
        for s in range(2):
            held = acc[s, g]
            out_ref[s, :, pl.ds(pl.multiple_of(g * DH, DH), DH)] = (held[:, :DH] / held[:, DH:]).astype(jnp.bfloat16)
        return carry

    lax.fori_loop(0, GROUPS, finish, 0)

    for name in TRANSFERS:
        copy_of(name).wait_send()
    for d in range(1, HEAD):
        for copy in cache_copies(d):
            copy.wait()


def body(queries, key_states, value_states, segment_ids):
    vmem = pl.BlockSpec(memory_space=pltpu.VMEM)
    count = len(TRANSFERS)
    return pl.pallas_call(
        kernel,
        out_shape=(
            jax.ShapeDtypeStruct((2, ROWS, GROUPS * DH), jnp.bfloat16),
            jax.ShapeDtypeStruct((CACHE, HEAD * DH), jnp.bfloat16),
            jax.ShapeDtypeStruct((CACHE, HEAD * DH), jnp.bfloat16),
        ),
        in_specs=[vmem] * 4,
        out_specs=(vmem,) * 3,
        scratch_shapes=[
            pltpu.VMEM((4, CTX, ROWS, DH), jnp.bfloat16),
            pltpu.VMEM((2 * CTX, ROWS, DH), jnp.bfloat16),
            pltpu.VMEM((2, GROUPS, ROWS, 2 * DH), jnp.bfloat16),
            pltpu.VMEM((2, GROUPS, ROWS, 2 * DH), jnp.float32),
            pltpu.VMEM((2, GROUPS, ROWS, DH), jnp.float32),
            pltpu.SemaphoreType.DMA((count,)),
            pltpu.SemaphoreType.DMA((count,)),
            pltpu.SemaphoreType.DMA((2, HEAD)),
            pltpu.SemaphoreType.DMA((2, HEAD)),
        ],
        compiler_params=pltpu.CompilerParams(
            collective_id=0, has_side_effects=True, vmem_limit_bytes=56 * 1024 * 1024
        ),
        name="attend_gather",
    )(queries, key_states, value_states, segment_ids.reshape(-1, DH))


def solution(mesh):
    in_specs = (P(None, "ctx", "head"), P(None, "ctx", "head"), P(None, "ctx", "head"), P())
    out_specs = (P(None, "ctx", "head"), P(("ctx", "head"), None), P(("ctx", "head"), None))
    return jax.shard_map(body, mesh=mesh, in_specs=in_specs, out_specs=out_specs, check_vma=False)
```

time: 365 us -> 68.6 us (0.19)
  the two profiles are of different devices: /device:TPU:205 before, /device:TPU:24 now
where the time goes in v1:
time: 68.6 us; the launch traced here: 67.7 us
  Pallas kernels  63.4 us (92%)
  local copies, waits for them, and re-layouts  3.67 us (5%)
    pallas_call x1, Pallas kernels, body(): pl.pallas_call(kernel, out_shape=(jax.ShapeDtypeStruct((2, ROWS, GROUPS *...  63.4 us
    unnamed x7, local copies, waits for them, and re-layouts  3.67 us

profile of v1, /device:TPU:24, one launch (start us, length us, event | category | flops | bytes accessed | tf_op | source)
XLA Modules:
  0.0 67.7 jit_solution(5048206196235343924)
XLA Ops:
  0.6 63.4 %attend_gather.1 = (bf16[2,192,1024]{2,1,0:T(8,128)(2,1)}, bf16[48,1024]{1,0:T(8,128)(2,1)}, bf16[48,1024]{1,0:T(8,128)(2,1)}) custom-call(bf16[2,192,1024]{2,1,0:T(8,128)(2,1)} %q_ref.1, bf16[2,192,128]{2,1,0:T(8,128)(2,1)} %k_ref.1, bf16[2,192,128]{2,1,0:T(8,128)(2,1)} %v_ref.1, s32[96,128]{1,0:T(8,128)} %bitcast.1), custom_call_target="tpu_custom_call" | custom-call | tf_op jit(solution)/shard_map/attend_gather/pallas_call | solution.py:351
  64.1 0.0 copy-start.1
  64.1 2.1 %copy.10 = bf16[2,192,1024]{2,1,0:T(8,128)(2,1)} copy(bf16[2,192,1024]{2,1,0:T(8,128)(2,1)} %get-tuple-element.6) | data formatting | bytes 1572864
  66.2 0.0 copy-done.1
  66.2 0.0 copy-start
  66.2 0.6 copy.11
  66.8 0.3 copy-done
  67.1 0.6 copy.12
Async XLA Ops:
  64.1 2.1 %copy-start.1 = (bf16[48,1024]{1,0:T(8,128)(2,1)S(1)}, bf16[48,1024]{1,0:T(8,128)(2,1)}, u32[]{:S(2)}) copy-start(bf16[48,1024]{1,0:T(8,128)(2,1)} %get-tuple-element.7) | copy-start | bytes 294916
  66.2 0.9 %copy-start = (bf16[48,1024]{1,0:T(8,128)(2,1)S(1)}, bf16[48,1024]{1,0:T(8,128)(2,1)}, u32[]{:S(2)}) copy-start(bf16[48,1024]{1,0:T(8,128)(2,1)} %get-tuple-element.8) | copy-start | bytes 294916

commit v2 on v1

--- a/solution.py
+++ b/solution.py
@@ -76,24 +76,24 @@
 OWN, NEAR, FAR, OPP = 0, 1, 2, 3
 PLAN = [
     2,
+    3,
     (OWN, 0, LOW),
-    3,
     (NEAR, 0, LOW),
     (NEAR, 0, HIGH),
+    (OWN, 1, LOW),
     4,
-    (OWN, 1, LOW),
     5,
     (FAR, 0, LOW),
     (FAR, 0, HIGH),
+    (NEAR, 1, LOW),
     6,
-    (NEAR, 1, LOW),
+    7,
     (OPP, 0, LOW),
-    7,
     (OPP, 0, HIGH),
     (FAR, 1, LOW),
     8,
+    9,
     (FAR, 1, HIGH),
-    9,
     (OPP, 1, LOW),
     (OWN, 1, HIGH),
     (NEAR, 1, HIGH),

time: 68.6 us -> 67.9 us (0.990)
  no operation moved by 1% of the time
where the time goes in v2:
time: 67.9 us; the launch traced here: 67.1 us
  Pallas kernels  62.8 us (92%)
  local copies, waits for them, and re-layouts  3.67 us (5%)
    pallas_call x1, Pallas kernels, body(): pl.pallas_call(kernel, out_shape=(jax.ShapeDtypeStruct((2, ROWS, GROUPS *...  62.8 us
    unnamed x7, local copies, waits for them, and re-layouts  3.67 us

profile of v2, /device:TPU:24, one launch (start us, length us, event | category | flops | bytes accessed | tf_op | source)
XLA Modules:
  0.0 67.1 jit_solution(9784204574214785773)
XLA Ops:
  0.6 62.8 %attend_gather.1 = (bf16[2,192,1024]{2,1,0:T(8,128)(2,1)}, bf16[48,1024]{1,0:T(8,128)(2,1)}, bf16[48,1024]{1,0:T(8,128)(2,1)}) custom-call(bf16[2,192,1024]{2,1,0:T(8,128)(2,1)} %q_ref.1, bf16[2,192,128]{2,1,0:T(8,128)(2,1)} %k_ref.1, bf16[2,192,128]{2,1,0:T(8,128)(2,1)} %v_ref.1, s32[96,128]{1,0:T(8,128)} %bitcast.1), custom_call_target="tpu_custom_call" | custom-call | tf_op jit(solution)/shard_map/attend_gather/pallas_call | solution.py:351
  63.5 0.0 copy-start.1
  63.5 2.1 %copy.10 = bf16[2,192,1024]{2,1,0:T(8,128)(2,1)} copy(bf16[2,192,1024]{2,1,0:T(8,128)(2,1)} %get-tuple-element.6) | data formatting | bytes 1572864
  65.6 0.0 copy-done.1
  65.6 0.0 copy-start
  65.6 0.6 copy.11
  66.2 0.3 copy-done
  66.5 0.6 copy.12
Async XLA Ops:
  63.5 2.1 %copy-start.1 = (bf16[48,1024]{1,0:T(8,128)(2,1)S(1)}, bf16[48,1024]{1,0:T(8,128)(2,1)}, u32[]{:S(2)}) copy-start(bf16[48,1024]{1,0:T(8,128)(2,1)} %get-tuple-element.7) | copy-start | bytes 294916
  65.6 0.9 %copy-start = (bf16[48,1024]{1,0:T(8,128)(2,1)S(1)}, bf16[48,1024]{1,0:T(8,128)(2,1)}, u32[]{:S(2)}) copy-start(bf16[48,1024]{1,0:T(8,128)(2,1)} %get-tuple-element.8) | copy-start | bytes 294916

commit v3 on v2

--- a/solution.py
+++ b/solution.py
@@ -59,7 +59,7 @@
 TRANSFERS = transfers()
 INDEX = {name: i for i, name in enumerate(TRANSFERS)}
 FORWARDS = {name: [k for k, v in TRANSFERS.items() if v[5] == name] for name in TRANSFERS}
-FIRST = [n + half + kv for half in "LH" for kv in "kv" for n in ("U1", "D1", "Y0", "C0")]
+ORDERS = (("up", "y", "down"), ("down", "up", "y"))
 
 ARRIVALS = [
     ["U1L", "D1L", "Y0L"],
@@ -177,14 +177,34 @@
             device_id_type=MESH,
         )
 
-    for name in FIRST:
-        copy_of(name).start()
+    def by_core(function):
+        for which, order in enumerate(ORDERS):
+            pl.when(core == which)(lambda order=order: function(order))
+
+    def link_order(names, order):
+        return sorted(names, key=lambda name: (name[-1], order.index(TRANSFERS[name][0]) if TRANSFERS[name][0] in order else 3))
+
+    @by_core
+    def _(order):
+        for half in "LH":
+            first = [n + half + kv for kv in "kv" for n in ("U1", "D1", "Y0")]
+            for name in link_order(first, order):
+                copy_of(name).start()
+            for kv in "kv":
+                copy_of("C0" + half + kv).start()
 
     def arrive(names):
-        for name in [n + kv for kv in "kv" for n in names]:
-            copy_of(name).wait_recv()
-            for onward in FORWARDS[name]:
-                copy_of(onward).start()
+        names = [n + kv for kv in "kv" for n in names]
+
+        @by_core
+        def _(order):
+            for name in link_order(names, order):
+                copy_of(name).wait_recv()
+                for onward in link_order(FORWARDS[name], order):
+                    if TRANSFERS[onward][0] != "core":
+                        copy_of(onward).start()
+            for name in names:
+                copy_of("C" + name).start()
 
     seg = seg_ref[...]
     lane = lax.broadcasted_iota(jnp.int32, (1, DH), 1)

time: 67.9 us -> 68.2 us (level)
  no operation moved by 1% of the time
where the time goes in v3:
time: 68.2 us; the launch traced here: 67.6 us
  Pallas kernels  63.3 us (93%)
  local copies, waits for them, and re-layouts  3.67 us (5%)
    pallas_call x1, Pallas kernels, body(): pl.pallas_call(kernel, out_shape=(jax.ShapeDtypeStruct((2, ROWS, GROUPS *...  63.3 us
    unnamed x7, local copies, waits for them, and re-layouts  3.67 us

profile of v3, /device:TPU:24, one launch (start us, length us, event | category | flops | bytes accessed | tf_op | source)
XLA Modules:
  0.0 67.6 jit_solution(7536556945186471608)
XLA Ops:
  0.6 63.3 %attend_gather.1 = (bf16[2,192,1024]{2,1,0:T(8,128)(2,1)}, bf16[48,1024]{1,0:T(8,128)(2,1)}, bf16[48,1024]{1,0:T(8,128)(2,1)}) custom-call(bf16[2,192,1024]{2,1,0:T(8,128)(2,1)} %q_ref.1, bf16[2,192,128]{2,1,0:T(8,128)(2,1)} %k_ref.1, bf16[2,192,128]{2,1,0:T(8,128)(2,1)} %v_ref.1, s32[96,128]{1,0:T(8,128)} %bitcast.1), custom_call_target="tpu_custom_call" | custom-call | tf_op jit(solution)/shard_map/attend_gather/pallas_call | solution.py:371
  64.0 0.0 copy-start.1
  64.0 2.1 %copy.10 = bf16[2,192,1024]{2,1,0:T(8,128)(2,1)} copy(bf16[2,192,1024]{2,1,0:T(8,128)(2,1)} %get-tuple-element.6) | data formatting | bytes 1572864
  66.1 0.0 copy-done.1
  66.1 0.0 copy-start
  66.1 0.6 copy.11
  66.7 0.3 copy-done
  67.0 0.6 copy.12
Async XLA Ops:
  64.0 2.1 %copy-start.1 = (bf16[48,1024]{1,0:T(8,128)(2,1)S(1)}, bf16[48,1024]{1,0:T(8,128)(2,1)}, u32[]{:S(2)}) copy-start(bf16[48,1024]{1,0:T(8,128)(2,1)} %get-tuple-element.7) | copy-start | bytes 294916
  66.1 0.9 %copy-start = (bf16[48,1024]{1,0:T(8,128)(2,1)S(1)}, bf16[48,1024]{1,0:T(8,128)(2,1)}, u32[]{:S(2)}) copy-start(bf16[48,1024]{1,0:T(8,128)(2,1)} %get-tuple-element.8) | copy-start | bytes 294916

commit v4 on v3

--- a/solution.py
+++ b/solution.py
@@ -15,7 +15,7 @@
 HEAD = 8
 KEYS = 4 * ROWS
 CACHE = 48
-TILE = 2
+TILE = 4
 OTHER = -(2.0 ** 20)
 LATER = -(2.0 ** 22)
 START = -(2.0 ** 23)
@@ -75,27 +75,25 @@
 ]
 OWN, NEAR, FAR, OPP = 0, 1, 2, 3
 PLAN = [
-    2,
-    3,
     (OWN, 0, LOW),
+    4,
+    5,
     (NEAR, 0, LOW),
     (NEAR, 0, HIGH),
     (OWN, 1, LOW),
-    4,
-    5,
+    6,
+    7,
     (FAR, 0, LOW),
     (FAR, 0, HIGH),
     (NEAR, 1, LOW),
-    6,
-    7,
+    8,
     (OPP, 0, LOW),
     (OPP, 0, HIGH),
     (FAR, 1, LOW),
-    8,
     9,
     (FAR, 1, HIGH),
+    (OWN, 1, HIGH),
     (OPP, 1, LOW),
-    (OWN, 1, HIGH),
     (NEAR, 1, HIGH),
     (OPP, 1, HIGH),
 ]
@@ -250,12 +248,17 @@
             row = lax.broadcasted_iota(jnp.int32, (ROWS, KEYS), 0) + at
             col = lax.broadcasted_iota(jnp.int32, (ROWS, KEYS), 1)
             seen = jnp.concatenate([row >= col] * TILE, axis=0)
-        for t in range(GROUPS // TILE):
-            heads = pl.ds(t * TILE, TILE)
-            queries = qx[qs, heads].reshape(rows, 2 * DH)
-            scores = lax.dot_general(
+        def scores_of(t):
+            queries = qx[qs, pl.ds(t * TILE, TILE)].reshape(rows, 2 * DH)
+            return lax.dot_general(
                 queries, keys, (((1,), (1,)), ((), ())), preferred_element_type=jnp.float32
             )
+
+        tiles = GROUPS // TILE
+        scores = scores_of(0)
+        for t in range(tiles):
+            later = scores_of(t + 1) if t + 1 < tiles else None
+            heads = pl.ds(t * TILE, TILE)
             if causal:
                 scores = jnp.where(seen, scores, LATER)
             parts = [scores[:, i * DH : (i + 1) * DH] for i in range(lanes)]
@@ -273,13 +276,14 @@
             held = held * jnp.concatenate([factor, factor], axis=1) + product
             acc[qs, heads] = held.reshape(TILE, ROWS, 2 * DH)
             peak[qs, heads] = new.reshape(TILE, ROWS, DH)
+            scores = later
 
     zb = z // 2
     own = y * 4 + zb
     toward = 1 - 2 * (z % 2)
 
-    arrive(ARRIVALS[0])
-    arrive(ARRIVALS[1])
+    for names in ARRIVALS[:4]:
+        arrive(names)
     for name in needs(OWN, 0, LOW) + needs(OWN, 0, HIGH):
         copy_of(name).wait_recv()
 

time: 68.2 us -> 64.9 us (0.952)
  Pallas kernels: 63.3 us -> 60.4 us
    pallas_call x1, Pallas kernels: 63.3 us -> 60.4 us  [body(): pl.pallas_call(kernel, out_shape=(jax.ShapeDtypeStruct((2, ROWS, GROUPS *...]
where the time goes in v4:
time: 64.9 us; the launch traced here: 64.8 us
  Pallas kernels  60.4 us (93%)
  local copies, waits for them, and re-layouts  3.67 us (6%)
  between operations  0.65 us (1%)
    pallas_call x1, Pallas kernels, body(): pl.pallas_call(kernel, out_shape=(jax.ShapeDtypeStruct((2, ROWS, GROUPS *...  60.4 us
    unnamed x7, local copies, waits for them, and re-layouts  3.67 us

profile of v4, /device:TPU:24, one launch (start us, length us, event | category | flops | bytes accessed | tf_op | source)
XLA Modules:
  0.0 64.8 jit_solution(10896588260260076192)
XLA Ops:
  0.6 60.4 %attend_gather.1 = (bf16[2,192,1024]{2,1,0:T(8,128)(2,1)}, bf16[48,1024]{1,0:T(8,128)(2,1)}, bf16[48,1024]{1,0:T(8,128)(2,1)}) custom-call(bf16[2,192,1024]{2,1,0:T(8,128)(2,1)} %q_ref.1, bf16[2,192,128]{2,1,0:T(8,128)(2,1)} %k_ref.1, bf16[2,192,128]{2,1,0:T(8,128)(2,1)} %v_ref.1, s32[96,128]{1,0:T(8,128)} %bitcast.1), custom_call_target="tpu_custom_call" | custom-call | tf_op jit(solution)/shard_map/attend_gather/pallas_call | solution.py:375
  61.1 0.0 copy-start.1
  61.1 2.1 %copy.10 = bf16[2,192,1024]{2,1,0:T(8,128)(2,1)} copy(bf16[2,192,1024]{2,1,0:T(8,128)(2,1)} %get-tuple-element.6) | data formatting | bytes 1572864
  63.2 0.0 copy-done.1
  63.2 0.0 copy-start
  63.2 0.6 copy.11
  63.8 0.3 copy-done
  64.1 0.6 copy.12
Async XLA Ops:
  61.1 2.1 %copy-start.1 = (bf16[48,1024]{1,0:T(8,128)(2,1)S(1)}, bf16[48,1024]{1,0:T(8,128)(2,1)}, u32[]{:S(2)}) copy-start(bf16[48,1024]{1,0:T(8,128)(2,1)} %get-tuple-element.7) | copy-start | bytes 294916
  63.2 0.9 %copy-start = (bf16[48,1024]{1,0:T(8,128)(2,1)S(1)}, bf16[48,1024]{1,0:T(8,128)(2,1)}, u32[]{:S(2)}) copy-start(bf16[48,1024]{1,0:T(8,128)(2,1)} %get-tuple-element.8) | copy-start | bytes 294916

commit v5 on v4

--- a/solution.py
+++ b/solution.py
@@ -59,6 +59,7 @@
 TRANSFERS = transfers()
 INDEX = {name: i for i, name in enumerate(TRANSFERS)}
 FORWARDS = {name: [k for k, v in TRANSFERS.items() if v[5] == name] for name in TRANSFERS}
+LATE, LATE_AFTER = ["YU1Hk", "YU1Hv", "YD1Hk", "YD1Hv"], 5
 ORDERS = (("up", "y", "down"), ("down", "up", "y"))
 
 ARRIVALS = [
@@ -75,26 +76,28 @@
 ]
 OWN, NEAR, FAR, OPP = 0, 1, 2, 3
 PLAN = [
+    2,
+    3,
     (OWN, 0, LOW),
+    (NEAR, 0, LOW),
+    (NEAR, 0, HIGH),
     4,
     5,
-    (NEAR, 0, LOW),
-    (NEAR, 0, HIGH),
     (OWN, 1, LOW),
+    (FAR, 0, LOW),
+    (FAR, 0, HIGH),
     6,
     7,
-    (FAR, 0, LOW),
-    (FAR, 0, HIGH),
     (NEAR, 1, LOW),
-    8,
     (OPP, 0, LOW),
     (OPP, 0, HIGH),
+    8,
     (FAR, 1, LOW),
+    (FAR, 1, HIGH),
     9,
-    (FAR, 1, HIGH),
     (OWN, 1, HIGH),
+    (NEAR, 1, HIGH),
     (OPP, 1, LOW),
-    (NEAR, 1, HIGH),
     (OPP, 1, HIGH),
 ]
 
@@ -191,16 +194,19 @@
             for kv in "kv":
                 copy_of("C0" + half + kv).start()
 
-    def arrive(names):
-        names = [n + kv for kv in "kv" for n in names]
+    def arrive(event):
+        names = [n + kv for kv in "kv" for n in ARRIVALS[event]]
 
         @by_core
         def _(order):
             for name in link_order(names, order):
                 copy_of(name).wait_recv()
                 for onward in link_order(FORWARDS[name], order):
-                    if TRANSFERS[onward][0] != "core":
+                    if TRANSFERS[onward][0] != "core" and onward not in LATE:
                         copy_of(onward).start()
+            if event == LATE_AFTER:
+                for name in LATE:
+                    copy_of(name).start()
             for name in names:
                 copy_of("C" + name).start()
 
@@ -282,8 +288,8 @@
     own = y * 4 + zb
     toward = 1 - 2 * (z % 2)
 
-    for names in ARRIVALS[:4]:
-        arrive(names)
+    arrive(0)
+    arrive(1)
     for name in needs(OWN, 0, LOW) + needs(OWN, 0, HIGH):
         copy_of(name).wait_recv()
 
@@ -307,7 +313,7 @@
                 @pl.when(step == i)
                 def _(events=events, names=names):
                     for event in events:
-                        arrive(ARRIVALS[event])
+                        arrive(event)
                     for name in names:
                         copy_of(name).wait_recv()
 

time: 64.9 us -> 64.1 us (0.988)
  Pallas kernels: 60.4 us -> 59.6 us
    pallas_call x1, Pallas kernels: 60.4 us -> 59.6 us  [body(): pl.pallas_call(kernel, out_shape=(jax.ShapeDtypeStruct((2, ROWS, GROUPS *...]
where the time goes in v5:
time: 64.1 us; the launch traced here: 63.9 us
  Pallas kernels  59.6 us (93%)
  local copies, waits for them, and re-layouts  3.67 us (6%)
  between operations  0.65 us (1%)
    pallas_call x1, Pallas kernels, body(): pl.pallas_call(kernel, out_shape=(jax.ShapeDtypeStruct((2, ROWS, GROUPS *...  59.6 us
    unnamed x7, local copies, waits for them, and re-layouts  3.67 us

profile of v5, /device:TPU:24, one launch (start us, length us, event | category | flops | bytes accessed | tf_op | source)
XLA Modules:
  0.0 63.9 jit_solution(10053160450587427792)
XLA Ops:
  0.6 59.6 %attend_gather.1 = (bf16[2,192,1024]{2,1,0:T(8,128)(2,1)}, bf16[48,1024]{1,0:T(8,128)(2,1)}, bf16[48,1024]{1,0:T(8,128)(2,1)}) custom-call(bf16[2,192,1024]{2,1,0:T(8,128)(2,1)} %q_ref.1, bf16[2,192,128]{2,1,0:T(8,128)(2,1)} %k_ref.1, bf16[2,192,128]{2,1,0:T(8,128)(2,1)} %v_ref.1, s32[96,128]{1,0:T(8,128)} %bitcast.1), custom_call_target="tpu_custom_call" | custom-call | tf_op jit(solution)/shard_map/attend_gather/pallas_call | solution.py:381
  60.2 0.0 copy-start.1
  60.3 2.1 %copy.10 = bf16[2,192,1024]{2,1,0:T(8,128)(2,1)} copy(bf16[2,192,1024]{2,1,0:T(8,128)(2,1)} %get-tuple-element.6) | data formatting | bytes 1572864
  62.4 0.0 copy-done.1
  62.4 0.0 copy-start
  62.4 0.6 %copy.11 = bf16[48,1024]{1,0:T(8,128)(2,1)} copy(bf16[48,1024]{1,0:T(8,128)(2,1)S(1)} %copy-done.1) | data formatting | bytes 196608
  63.0 0.3 copy-done
  63.3 0.6 %copy.12 = bf16[48,1024]{1,0:T(8,128)(2,1)} copy(bf16[48,1024]{1,0:T(8,128)(2,1)S(1)} %copy-done) | data formatting | bytes 196608
Async XLA Ops:
  60.2 2.1 %copy-start.1 = (bf16[48,1024]{1,0:T(8,128)(2,1)S(1)}, bf16[48,1024]{1,0:T(8,128)(2,1)}, u32[]{:S(2)}) copy-start(bf16[48,1024]{1,0:T(8,128)(2,1)} %get-tuple-element.7) | copy-start | bytes 294916
  62.4 0.9 %copy-start = (bf16[48,1024]{1,0:T(8,128)(2,1)S(1)}, bf16[48,1024]{1,0:T(8,128)(2,1)}, u32[]{:S(2)}) copy-start(bf16[48,1024]{1,0:T(8,128)(2,1)} %get-tuple-element.8) | copy-start | bytes 294916

commit v6 on v2

v6 whole, which is shorter than its diff:
```python
import math

import jax
import jax.numpy as jnp
from jax import lax
from jax.experimental import pallas as pl
from jax.experimental.pallas import tpu as pltpu
from jax.sharding import PartitionSpec as P

MESH = pl.DeviceIdType.MESH
DH = 128
GROUPS = 8
ROWS = 192
CTX = 32
HEAD = 8
KEYS = 4 * ROWS
CACHE = 48
TILE = 2
OTHER = -(2.0 ** 20)
LATER = -(2.0 ** 22)
LARGEST = 1e30
START = -(2.0 ** 23)
SCALE = 1.0 / math.sqrt(DH)

LOW, HIGH = 0, 1
PARTS = 2
PIECES = range(2 * PARTS)
GATHER_VMEM = 16 * 1024 * 1024
ATTEND_VMEM = 40 * 1024 * 1024


def transfers():
    out = {}

    def add(name, link, row, dz, half, source):
        out[name] = (link, row, dz, half, source)

    for half, tag in ((LOW, "L"), (HIGH, "H")):
        for d in (1, 2, 3):
            add(f"U{d}{tag}", "up", 0, -d, half, f"U{d - 1}{tag}" if d > 1 else None)
            add(f"D{d}{tag}", "down", 0, d, half, f"D{d - 1}{tag}" if d > 1 else None)
        add(f"Y0{tag}", "y", 1, 0, half, None)
        for d in (1, 2):
            add(f"YU{d}{tag}", "y", 1, -d, half, f"U{d}{tag}")
            add(f"YD{d}{tag}", "y", 1, d, half, f"D{d}{tag}")
        add(f"OU3{tag}", "up", 1, -3, half, f"YU2{tag}")
        add(f"OD3{tag}", "down", 1, 3, half, f"YD2{tag}")
    add("U4L", "up", 0, -4, LOW, "U3L")
    add("D4H", "down", 0, 4, HIGH, "D3H")
    add("OU4L", "up", 1, -4, LOW, "OU3L")
    add("OD4H", "down", 1, 4, HIGH, "OD3H")
    for name in list(out):
        link, row, dz, half, source = out[name]
        add("C" + name, "core", row, dz, half, name)
    add("C0L", "core", 0, 0, LOW, None)
    add("C0H", "core", 0, 0, HIGH, None)
    return {
        f"{name}{tag}": (link, row, dz, half, tag, source and f"{source}{tag}")
        for name, (link, row, dz, half, source) in out.items()
        for tag in PIECES
    }


TRANSFERS = transfers()
INDEX = {name: i for i, name in enumerate(TRANSFERS)}
FORWARDS = {name: [k for k, v in TRANSFERS.items() if v[5] == name] for name in TRANSFERS}
FIRST = [f"{n}{half}{p}" for half in "LH" for p in PIECES for n in ("U1", "D1", "Y0")]
FIRST += [f"C0{half}{p}" for half in "LH" for p in PIECES]

ARRIVALS = [
    ["U1L", "D1L", "Y0L"],
    ["U1H", "D1H", "Y0H"],
    ["U2L", "D2L", "YU1L"],
    ["U2H", "D2H", "YD1L"],
    ["U3L", "D3L", "YU2L"],
    ["U3H", "D3H", "YD2L"],
    ["U4L", "D4H", "YU2H"],
    ["OU3L", "OD3L", "YD2H"],
    ["OU3H", "OD3H", "YU1H"],
    ["OU4L", "OD4H", "YD1H"],
]
LATE, LATE_AFTER = [f"{n}{p}" for p in PIECES for n in ("YU1H", "YD1H")], 5


def gather_kernel(k_ref, v_ref, buf, kc_ref, vc_ref, send, recv, csend, crecv, own):
    c = lax.axis_index("ctx")
    h = lax.axis_index("head")
    y, z, core = c // 16, (c % 16) // 2, c % 2

    def index_of(row, zz, kk):
        return row * 16 + (zz % 8) * 2 + kk

    up_to = index_of(y, z + 1, core)
    down_to = index_of(y, z + 7, core)
    y_to = index_of(1 - y, z, core)
    core_to = index_of(y, z, 1 - core)
    target = {"up": up_to, "down": down_to, "y": y_to, "core": core_to}

    barrier = pltpu.get_barrier_semaphore()
    for peer in (up_to, down_to, y_to, core_to):
        pl.semaphore_signal(barrier, inc=1, device_id=(peer, h), device_id_type=MESH)
    for d in range(1, HEAD):
        pl.semaphore_signal(barrier, inc=1, device_id=(c, (h + d) % HEAD), device_id_type=MESH)
    own_copies = [
        pltpu.make_async_copy((k_ref, v_ref)[kv].at[half], buf.at[2 * half + kv, c], own.at[2 * half + kv])
        for half in range(2)
        for kv in range(2)
    ]
    for copy in own_copies:
        copy.start()
    pl.semaphore_wait(barrier, 4 + HEAD - 1)

    def copy_of(name):
        link, row, dz, half, piece, source = TRANSFERS[name]
        shift = {"up": 1, "down": -1}.get(link, 0)
        there = y if (row == 0) != (link == "y") else 1 - y
        block = index_of(there, z + dz + shift + 8, core)
        part = pl.ds(piece % PARTS * (ROWS // PARTS), ROWS // PARTS)
        dst = buf.at[2 * half + piece // PARTS, block, part]
        return pltpu.make_async_remote_copy(
            src_ref=dst if source else (k_ref, v_ref)[piece // PARTS].at[half, part],
            dst_ref=dst,
            send_sem=send.at[0],
            recv_sem=recv.at[INDEX[name]],
            device_id=(target[link], h),
            device_id_type=MESH,
        )

    for name in FIRST:
        copy_of(name).start()

    for event, names in enumerate(ARRIVALS):
        names = [f"{n}{p}" for p in PIECES for n in names]
        for name in names:
            copy_of(name).wait_recv()
            for onward in FORWARDS[name]:
                if TRANSFERS[onward][0] != "core" and onward not in LATE:
                    copy_of(onward).start()
        for name in names:
            copy_of("C" + name).start()
        if event == LATE_AFTER:
            for name in LATE:
                copy_of(name).start()
    for name in TRANSFERS:
        if TRANSFERS[name][0] == "core":
            copy_of(name).wait_recv()
    for copy in own_copies:
        copy.wait()

    page = c // 16
    columns = pl.ds(pl.multiple_of(h * DH, DH), DH)

    def cache_source(kv, to):
        return buf.at[2 * page + kv, 2 * (c % 16) + to // 4, pl.ds(pl.multiple_of(CACHE * (to % 4), 16), CACHE)]

    def cache_copies(d):
        to = (h + d) % HEAD
        return [
            pltpu.make_async_remote_copy(
                src_ref=cache_source(kv, to),
                dst_ref=ref.at[:, columns],
                send_sem=csend.at[kv, d],
                recv_sem=crecv.at[kv, d],
                device_id=(c, to),
                device_id_type=MESH,
            )
            for kv, ref in ((0, kc_ref), (1, vc_ref))
        ]

    for d in range(1, HEAD):
        for copy in cache_copies(d):
            copy.start()
    mine = [
        pltpu.make_async_copy(cache_source(kv, h), ref.at[:, columns], own.at[kv])
        for kv, ref in ((0, kc_ref), (1, vc_ref))
    ]
    for copy in mine:
        copy.start()

    sent = buf.at[:, pl.ds(0, len(TRANSFERS) // (4 * PARTS))]
    pltpu.make_async_remote_copy(
        src_ref=sent, dst_ref=sent, send_sem=send.at[0], recv_sem=recv.at[0], device_id=(core_to, h), device_id_type=MESH
    ).wait_send()
    for copy in mine:
        copy.wait()
    for d in range(1, HEAD):
        for copy in cache_copies(d):
            copy.wait()


def attend_kernel(q_ref, seg_ref, kin_ref, vin_ref, buf, out_ref, kc_ref, vc_ref, qx, acc, peak, state):
    c = lax.axis_index("ctx")
    kc_ref[...] = kin_ref[...]
    vc_ref[...] = vin_ref[...]

    seg = seg_ref[...]
    starts = [jnp.int32(0)] + [
        jnp.sum(jnp.where(seg < s, 1.0, 0.0)).astype(jnp.int32) for s in range(1, 4)
    ] + [jnp.int32(2 * CTX * ROWS)]
    lane = lax.broadcasted_iota(jnp.int32, (1, DH), 1)
    low = jnp.zeros((1, DH), jnp.int32)
    high = jnp.zeros((1, DH), jnp.int32)
    for s in range(4):
        low = jnp.where(lane == s, starts[s], low)
        high = jnp.where(lane == s, starts[s + 1], high)
    used = jnp.where(lane < 4, 1.0, 0.0)

    def inside(first, rows):
        at = lax.broadcasted_iota(jnp.int32, (rows, DH), 0) + first
        return jnp.where(jnp.logical_and(at >= low, at < high), 1.0, 0.0)

    def segment_start(at):
        begin = jnp.int32(0)
        for start in starts[1:4]:
            begin = jnp.where(start <= at, start, begin)
        return begin

    own, first_block, inner = [], [], []
    for s in range(2):
        at = s * CTX * ROWS + c * ROWS
        own.append(at // KEYS)
        first_block.append(segment_start(at) // KEYS)
        inner.append(segment_start(at + ROWS - 1))
    count = own[0] - first_block[0] + 1
    total = count + own[1] - first_block[1] + 1

    for s in range(2):
        feature = ((used - inside(s * CTX * ROWS + c * ROWS, ROWS)) * OTHER).astype(jnp.bfloat16)
        for g in range(GROUPS):
            qx[s, g, :, :DH] = q_ref[s, :, g * DH : (g + 1) * DH]
            qx[s, g, :, DH:] = feature
    peak[...] = jnp.full(peak.shape, START, jnp.float32)
    acc[0] = jnp.zeros(acc.shape[1:], jnp.float32)
    state[0] = 0
    state[1] = 0

    rows = TILE * ROWS
    lanes = KEYS // DH
    ones = jnp.ones((KEYS, DH), jnp.bfloat16)

    def operands(block, featured):
        half, chunk = block // 8, (block % 8) * 4
        keys = buf[2 * half, pl.ds(chunk, 4)].reshape(KEYS, DH)
        values = buf[2 * half + 1, pl.ds(chunk, 4)].reshape(KEYS, DH)
        if featured:
            keys = jnp.concatenate([keys, inside(block * KEYS, KEYS).astype(jnp.bfloat16)], axis=1)
        return keys, values

    def scores_of(qs, t, keys):
        width = keys.shape[1]
        queries = qx[qs, pl.ds(t * TILE, TILE), :, :width].reshape(rows, width)
        return lax.dot_general(queries, keys, (((1,), (1,)), ((), ())), preferred_element_type=jnp.float32)

    tiles = GROUPS // TILE

    def attend(qs, block):
        keys, values = operands(block, True)
        now = state[qs]
        at = c * ROWS + qs * CTX * ROWS - block * KEYS
        key_row = lax.broadcasted_iota(jnp.int32, (KEYS, DH), 0)
        values = jnp.where(key_row < at + ROWS, values, jnp.zeros_like(values))
        values = jnp.concatenate([values, ones], axis=1)
        row = lax.broadcasted_iota(jnp.int32, (ROWS, KEYS), 0) + at
        col = lax.broadcasted_iota(jnp.int32, (ROWS, KEYS), 1)
        seen = jnp.concatenate([row >= col] * TILE, axis=0)
        scores = scores_of(qs, 0, keys)
        for t in range(tiles):
            later = scores_of(qs, t + 1, keys) if t + 1 < tiles else None
            heads = pl.ds(t * TILE, TILE)
            scores = jnp.where(seen, scores, LATER)
            parts = [scores[:, i * DH : (i + 1) * DH] for i in range(lanes)]
            top = parts[0]
            for part in parts[1:]:
                top = jnp.maximum(top, part)
            old = peak[qs, heads].reshape(rows, DH)
            new = jnp.maximum(old, jnp.max(top, axis=1, keepdims=True))
            weights = jnp.concatenate(
                [jnp.exp((part - new) * SCALE).astype(jnp.bfloat16) for part in parts], axis=1
            )
            factor = jnp.exp((old - new) * SCALE)
            product = jnp.dot(weights, values, preferred_element_type=jnp.float32)
            held = acc[now, qs, heads].reshape(rows, 2 * DH)
            held = held * jnp.concatenate([factor, factor], axis=1) + product
            acc[now, qs, heads] = held.reshape(TILE, ROWS, 2 * DH)
            peak[qs, heads] = new.reshape(TILE, ROWS, DH)
            scores = later

    def attend_kept(qs, block, featured):
        keys, values = operands(block, featured)
        values = jnp.concatenate([values, ones], axis=1)
        now = state[qs]
        scores = scores_of(qs, 0, keys)
        largest = jnp.zeros((8, DH), jnp.float32)
        for t in range(tiles):
            later = scores_of(qs, t + 1, keys) if t + 1 < tiles else None
            heads = pl.ds(t * TILE, TILE)
            top = peak[qs, heads].reshape(rows, DH)
            weights = jnp.concatenate(
                [
                    jnp.exp((scores[:, i * DH : (i + 1) * DH] - top) * SCALE).astype(jnp.bfloat16)
                    for i in range(lanes)
                ],
                axis=1,
            )
            product = jnp.dot(weights, values, preferred_element_type=jnp.float32)
            held = acc[now, qs, heads].reshape(rows, 2 * DH) + product
            acc[1 - now, qs, heads] = held.reshape(TILE, ROWS, 2 * DH)
            largest = jnp.maximum(largest, jnp.max(held[:, DH:].reshape(rows // 8, 8, DH), axis=0))
            scores = later
        fits = jnp.max(largest) <= LARGEST
        state[qs] = jnp.where(fits, 1 - now, now)
        state[2] = jnp.where(fits, 0, 1)

    def step(j, carry):
        upper = j >= count
        qs = jnp.where(upper, 1, 0)
        mine = jnp.where(upper, own[1], own[0])
        block = mine - jnp.where(upper, j - count, j)
        plain = block * KEYS >= jnp.where(upper, inner[1], inner[0])
        state[2] = jnp.where(block == mine, 1, 0)

        @pl.when(jnp.logical_and(block < mine, plain))
        def _():
            attend_kept(qs, block, False)

        @pl.when(jnp.logical_and(block < mine, jnp.logical_not(plain)))
        def _():
            attend_kept(qs, block, True)

        @pl.when(state[2] == 1)
        def _():
            attend(qs, block)

        return carry

    lax.fori_loop(0, total, step, 0)

    def finish(g, carry):
        for s in range(2):
            held = acc[state[s], s, g]
            out_ref[s, :, pl.ds(pl.multiple_of(g * DH, DH), DH)] = (held[:, :DH] / held[:, DH:]).astype(jnp.bfloat16)
        return carry

    lax.fori_loop(0, GROUPS, finish, 0)


def body(queries, key_states, value_states, segment_ids):
    vmem = pl.BlockSpec(memory_space=pltpu.VMEM)
    anywhere = pl.BlockSpec(memory_space=pl.ANY)
    cache = jax.ShapeDtypeStruct((CACHE, HEAD * DH), jnp.bfloat16)
    gathered, keys, values = pl.pallas_call(
        gather_kernel,
        out_shape=(jax.ShapeDtypeStruct((4, CTX, ROWS, DH), jnp.bfloat16), cache, cache),
        in_specs=[anywhere] * 2,
        out_specs=(anywhere,) * 3,
        scratch_shapes=[
            pltpu.SemaphoreType.DMA((1,)),
            pltpu.SemaphoreType.DMA((len(TRANSFERS),)),
            pltpu.SemaphoreType.DMA((2, HEAD)),
            pltpu.SemaphoreType.DMA((2, HEAD)),
            pltpu.SemaphoreType.DMA((4,)),
        ],
        compiler_params=pltpu.CompilerParams(
            collective_id=0, has_side_effects=True, vmem_limit_bytes=GATHER_VMEM
        ),
        name="gather",
    )(key_states, value_states)
    return pl.pallas_call(
        attend_kernel,
        out_shape=(jax.ShapeDtypeStruct((2, ROWS, GROUPS * DH), jnp.bfloat16), cache, cache),
        in_specs=[vmem] * 5,
        out_specs=(vmem,) * 3,
        scratch_shapes=[
            pltpu.VMEM((2, GROUPS, ROWS, 2 * DH), jnp.bfloat16),
            pltpu.VMEM((2, 2, GROUPS, ROWS, 2 * DH), jnp.float32),
            pltpu.VMEM((2, GROUPS, ROWS, DH), jnp.float32),
            pltpu.SMEM((3,), jnp.int32),
        ],
        compiler_params=pltpu.CompilerParams(vmem_limit_bytes=ATTEND_VMEM),
        name="attend",
    )(queries, segment_ids.reshape(-1, DH), keys, values, gathered)


def solution(mesh):
    in_specs = (P(None, "ctx", "head"), P(None, "ctx", "head"), P(None, "ctx", "head"), P())
    out_specs = (P(None, "ctx", "head"), P(("ctx", "head"), None), P(("ctx", "head"), None))
    return jax.shard_map(body, mesh=mesh, in_specs=in_specs, out_specs=out_specs, check_vma=False)
```

time: 67.9 us -> 76.1 us (1.12)
  the two profiles are of different devices: /device:TPU:24 before, /device:TPU:56 now
where the time goes in v6:
time: 76.1 us; the launch traced here: 75.9 us
  Pallas kernels  71.5 us (94%)
  local copies, waits for them, and re-layouts  3.7 us (5%)
    pallas_call x1, Pallas kernels, body(): pl.pallas_call(gather_kernel, out_shape=(jax.ShapeDtypeStruct((4, CTX, RO...  43.2 us
    pallas_call x1, Pallas kernels, body(): pl.pallas_call(attend_kernel, out_shape=(jax.ShapeDtypeStruct((2, ROWS, G...  28.4 us
    unnamed x8, local copies, waits for them, and re-layouts  3.7 us

profile of v6, /device:TPU:56, one launch (start us, length us, event | category | flops | bytes accessed | tf_op | source)
XLA Modules:
  0.0 75.9 jit_solution(13887335143053733114)
XLA Ops:
  0.6 0.0 copy-start.1
  0.6 0.9 %copy-done.1 = bf16[2,192,128]{2,1,0:T(8,128)(2,1)S(1)} copy-done((bf16[2,192,128]{2,1,0:T(8,128)(2,1)S(1)}, bf16[2,192,128]{2,1,0:T(8,128)(2,1)}, u32[]{:S(2)}) %copy-start.1) | copy-done | bytes 98328
  1.5 0.0 copy-start.2
  1.5 0.9 %copy-done.2 = bf16[2,192,128]{2,1,0:T(8,128)(2,1)S(1)} copy-done((bf16[2,192,128]{2,1,0:T(8,128)(2,1)S(1)}, bf16[2,192,128]{2,1,0:T(8,128)(2,1)}, u32[]{:S(2)}) %copy-start.2) | copy-done | bytes 98328
  2.4 43.2 %gather.1 = (bf16[4,32,192,128]{3,2,1,0:T(8,128)(2,1)S(1)}, bf16[48,1024]{1,0:T(8,128)(2,1)S(1)}, bf16[48,1024]{1,0:T(8,128)(2,1)S(1)}) custom-call(bf16[2,192,128]{2,1,0:T(8,128)(2,1)S(1)} %copy-done.1, bf16[2,192,128]{2,1,0:T(8,128)(2,1)S(1)} %copy-done.2), custom_call_target="tpu_custom_call" | custom-call | tf_op jit(solution)/shard_map/gather/pallas_call | solution.py:351
  45.6 0.0 copy-start
  45.6 1.1 %copy-done = bf16[2,192,1024]{2,1,0:T(8,128)(2,1)S(1)} copy-done((bf16[2,192,1024]{2,1,0:T(8,128)(2,1)S(1)}, bf16[2,192,1024]{2,1,0:T(8,128)(2,1)}, u32[]{:S(2)}) %copy-start) | copy-done | bytes 786456
  46.7 0.0 copy-start.3
  46.7 0.8 %copy-done.3 = s32[12288]{0:T(1024)S(1)} copy-done((s32[12288]{0:T(1024)S(1)}, s32[12288]{0:T(1024)}, u32[]{:S(2)}) %copy-start.3) | copy-done | bytes 49176
  47.5 28.4 %attend.1 = (bf16[2,192,1024]{2,1,0:T(8,128)(2,1)}, bf16[48,1024]{1,0:T(8,128)(2,1)}, bf16[48,1024]{1,0:T(8,128)(2,1)}) custom-call(bf16[2,192,1024]{2,1,0:T(8,128)(2,1)S(1)} %copy-done, s32[96,128]{1,0:T(8,128)S(1)} %bitcast.1, bf16[48,1024]{1,0:T(8,128)(2,1)S(1)} %get-tuple-element.6.kin_ref, bf16[48,1024]{1,0:T(8,128)(2,1)S(1)} %get-tuple-element.7.vin_ref, ...), custom_call_target="tpu_custom_call" | custom-call | tf_op jit(solution)/shard_map/attend/pallas_call | solution.py:368
Async XLA Ops:
  0.6 0.9 %copy-start.1 = (bf16[2,192,128]{2,1,0:T(8,128)(2,1)S(1)}, bf16[2,192,128]{2,1,0:T(8,128)(2,1)}, u32[]{:S(2)}) copy-start(bf16[2,192,128]{2,1,0:T(8,128)(2,1)} %k_ref.1) | copy-start | bytes 294916
  1.5 0.9 %copy-start.2 = (bf16[2,192,128]{2,1,0:T(8,128)(2,1)S(1)}, bf16[2,192,128]{2,1,0:T(8,128)(2,1)}, u32[]{:S(2)}) copy-start(bf16[2,192,128]{2,1,0:T(8,128)(2,1)} %v_ref.1) | copy-start | bytes 294916
  45.6 1.1 %copy-start = (bf16[2,192,1024]{2,1,0:T(8,128)(2,1)S(1)}, bf16[2,192,1024]{2,1,0:T(8,128)(2,1)}, u32[]{:S(2)}) copy-start(bf16[2,192,1024]{2,1,0:T(8,128)(2,1)} %q_ref.1) | copy-start | bytes 2359300
  46.7 0.8 %copy-start.3 = (s32[12288]{0:T(1024)S(1)}, s32[12288]{0:T(1024)}, u32[]{:S(2)}) copy-start(s32[12288]{0:T(1024)} %param.7) | copy-start | bytes 147460

commit v7 on v6

--- a/solution.py
+++ b/solution.py
@@ -15,7 +15,7 @@
 HEAD = 8
 KEYS = 4 * ROWS
 CACHE = 48
-TILE = 2
+TILE = 4
 OTHER = -(2.0 ** 20)
 LATER = -(2.0 ** 22)
 LARGEST = 1e30
@@ -23,10 +23,10 @@
 SCALE = 1.0 / math.sqrt(DH)
 
 LOW, HIGH = 0, 1
-PARTS = 2
+PARTS = 1
 PIECES = range(2 * PARTS)
-GATHER_VMEM = 16 * 1024 * 1024
-ATTEND_VMEM = 40 * 1024 * 1024
+GATHER_VMEM = 36 * 1024 * 1024
+ATTEND_VMEM = 36 * 1024 * 1024
 
 
 def transfers():
@@ -81,8 +81,50 @@
 ]
 LATE, LATE_AFTER = [f"{n}{p}" for p in PIECES for n in ("YU1H", "YD1H")], 5
 
-
-def gather_kernel(k_ref, v_ref, buf, kc_ref, vc_ref, send, recv, csend, crecv, own):
+OWN, NEAR, FAR, OPP = 0, 1, 2, 3
+PLAN = [2, 3, (NEAR, LOW), (NEAR, HIGH), 4, 5, (FAR, LOW), (FAR, HIGH), 6, 7, (OPP, LOW), (OPP, HIGH)]
+REACH = {OWN: (0, 1), NEAR: (1, 2), FAR: (2, 3), OPP: (3, 4)}
+
+
+def needs(kind, half):
+    return [
+        name
+        for name, (link, r, dz, hf, _, _) in TRANSFERS.items()
+        if link == "core" and r == 0 and hf == half and abs(dz) in REACH[kind]
+    ]
+
+
+def steps_of(plan):
+    jobs, before, pending, seen = [], [], [], set(needs(OWN, LOW) + needs(OWN, HIGH))
+    for entry in plan:
+        if isinstance(entry, int):
+            pending.append(entry)
+        else:
+            jobs.append(entry)
+            fresh = [name for name in needs(*entry) if name not in seen]
+            seen.update(fresh)
+            before.append((pending, fresh))
+            pending = []
+    rest = [name for name in TRANSFERS if TRANSFERS[name][0] == "core" and name not in seen]
+    return jobs, before, rest
+
+
+JOBS, BEFORE, REST = steps_of(PLAN)
+
+
+def online(scores, old, held, values):
+    parts = [scores[:, i : i + DH] for i in range(0, KEYS, DH)]
+    top = parts[0]
+    for part in parts[1:]:
+        top = jnp.maximum(top, part)
+    new = jnp.maximum(old, jnp.max(top, axis=1, keepdims=True))
+    weights = jnp.concatenate([jnp.exp((part - new) * SCALE).astype(jnp.bfloat16) for part in parts], axis=1)
+    factor = jnp.exp((old - new) * SCALE)
+    product = jnp.dot(weights, values, preferred_element_type=jnp.float32)
+    return new, held * jnp.concatenate([factor, factor], axis=1) + product
+
+
+def gather_kernel(q_ref, k_ref, v_ref, seg_ref, buf, kc_ref, vc_ref, qx, acc, peak, send, recv, csend, crecv, own):
     c = lax.axis_index("ctx")
     h = lax.axis_index("head")
     y, z, core = c // 16, (c % 16) // 2, c % 2
@@ -101,13 +143,9 @@
         pl.semaphore_signal(barrier, inc=1, device_id=(peer, h), device_id_type=MESH)
     for d in range(1, HEAD):
         pl.semaphore_signal(barrier, inc=1, device_id=(c, (h + d) % HEAD), device_id_type=MESH)
-    own_copies = [
-        pltpu.make_async_copy((k_ref, v_ref)[kv].at[half], buf.at[2 * half + kv, c], own.at[2 * half + kv])
-        for half in range(2)
-        for kv in range(2)
-    ]
-    for copy in own_copies:
-        copy.start()
+    for half in range(2):
+        buf[2 * half, c] = k_ref[half]
+        buf[2 * half + 1, c] = v_ref[half]
     pl.semaphore_wait(barrier, 4 + HEAD - 1)
 
     def copy_of(name):
@@ -118,7 +156,7 @@
         part = pl.ds(piece % PARTS * (ROWS // PARTS), ROWS // PARTS)
         dst = buf.at[2 * half + piece // PARTS, block, part]
         return pltpu.make_async_remote_copy(
-            src_ref=dst if source else (k_ref, v_ref)[piece // PARTS].at[half, part],
+            src_ref=dst,
             dst_ref=dst,
             send_sem=send.at[0],
             recv_sem=recv.at[INDEX[name]],
@@ -129,8 +167,8 @@
     for name in FIRST:
         copy_of(name).start()
 
-    for event, names in enumerate(ARRIVALS):
-        names = [f"{n}{p}" for p in PIECES for n in names]
+    def arrive(event):
+        names = [f"{n}{p}" for p in PIECES for n in ARRIVALS[event]]
         for name in names:
             copy_of(name).wait_recv()
             for onward in FORWARDS[name]:
@@ -141,11 +179,115 @@
         if event == LATE_AFTER:
             for name in LATE:
                 copy_of(name).start()
-    for name in TRANSFERS:
-        if TRANSFERS[name][0] == "core":
-            copy_of(name).wait_recv()
-    for copy in own_copies:
-        copy.wait()
+
+    seg = seg_ref[...]
+    lane = lax.broadcasted_iota(jnp.int32, (1, DH), 1)
+    low = jnp.zeros((1, DH), jnp.float32)
+    high = jnp.zeros((1, DH), jnp.float32)
+    for s in range(4):
+        below = jnp.sum(jnp.where(seg < s, 1.0, 0.0), axis=(0, 1), keepdims=True)
+        upto = jnp.sum(jnp.where(seg <= s, 1.0, 0.0), axis=(0, 1), keepdims=True)
+        low = jnp.where(lane == s, below, low)
+        high = jnp.where(lane == s, upto, high)
+    used = jnp.where(lane < 4, 1.0, 0.0)
+
+    def inside(first, rows):
+        at = (lax.broadcasted_iota(jnp.int32, (rows, DH), 0) + first).astype(jnp.float32)
+        return jnp.where((at >= low) & (at < high), 1.0, 0.0)
+
+    for s in range(2):
+        feature = ((used - inside(s * CTX * ROWS + c * ROWS, ROWS)) * OTHER).astype(jnp.bfloat16)
+        for g in range(GROUPS):
+            qx[s, g, :, :DH] = q_ref[s, :, g * DH : (g + 1) * DH]
+            qx[s, g, :, DH:] = feature
+    peak[...] = jnp.full(peak.shape, START, jnp.float32)
+    acc[...] = jnp.zeros(acc.shape, jnp.float32)
+
+    rows = TILE * ROWS
+    ones = jnp.ones((KEYS, DH), jnp.bfloat16)
+
+    def attend(qs, half, block, causal):
+        first = block * 4
+        keys = buf[2 * half, pl.ds(first, 4)].reshape(KEYS, DH)
+        values = buf[2 * half + 1, pl.ds(first, 4)].reshape(KEYS, DH)
+        features = inside((half * CTX + first) * ROWS, KEYS).astype(jnp.bfloat16)
+        keys = jnp.concatenate([keys, features], axis=1)
+        values = jnp.concatenate([values, ones], axis=1)
+        seen = None
+        if causal:
+            row = lax.broadcasted_iota(jnp.int32, (ROWS, KEYS), 0) + (c - first) * ROWS
+            col = lax.broadcasted_iota(jnp.int32, (ROWS, KEYS), 1)
+            seen = jnp.concatenate([row >= col] * TILE, axis=0)
+
+        def scores_of(t):
+            queries = qx[qs, pl.ds(t * TILE, TILE)].reshape(rows, 2 * DH)
+            return lax.dot_general(
+                queries, keys, (((1,), (1,)), ((), ())), preferred_element_type=jnp.float32
+            )
+
+        scores = scores_of(0)
+        for t in range(GROUPS // TILE):
+            later = scores_of(t + 1) if t + 1 < GROUPS // TILE else None
+            heads = pl.ds(t * TILE, TILE)
+            if causal:
+                scores = jnp.where(seen, scores, LATER)
+            old = peak[qs, heads].reshape(rows, DH)
+            held = acc[qs, heads].reshape(rows, 2 * DH)
+            new, held = online(scores, old, held, values)
+            acc[qs, heads] = held.reshape(TILE, ROWS, 2 * DH)
+            peak[qs, heads] = new.reshape(TILE, ROWS, DH)
+            scores = later
+
+    zb = z // 2
+    mine = y * 4 + zb
+    toward = 1 - 2 * (z % 2)
+
+    arrive(0)
+    arrive(1)
+    for name in needs(OWN, LOW) + needs(OWN, HIGH):
+        copy_of(name).wait_recv()
+
+    def own_step(half, carry):
+        attend(half, half, mine, True)
+        return carry
+
+    lax.fori_loop(0, 2, own_step, 0)
+
+    def step_body(step, carry):
+        def pick(values):
+            value = jnp.int32(values[0])
+            for i in range(1, len(values)):
+                value = jnp.where(step == i, jnp.int32(values[i]), value)
+            return value
+
+        for i, (events, names) in enumerate(BEFORE):
+            if events or names:
+
+                @pl.when(step == i)
+                def _(events=events, names=names):
+                    for event in events:
+                        arrive(event)
+                    for name in names:
+                        copy_of(name).wait_recv()
+
+        half = pick([job[1] for job in JOBS])
+        move = pick([{NEAR: 0, FAR: 0, OPP: 2}[job[0]] for job in JOBS]) + toward * pick(
+            [{NEAR: -1, FAR: 1, OPP: 0}[job[0]] for job in JOBS]
+        )
+        block = y * 4 + (zb + move + 4) % 4
+        qs = jnp.where(jnp.logical_or(half == 1, block > mine), 1, 0)
+
+        @pl.when(jnp.logical_or(half == 0, block < mine))
+        def _():
+            attend(qs, half, block, False)
+
+        return carry
+
+    lax.fori_loop(0, len(JOBS), step_body, 0)
+    arrive(8)
+    arrive(9)
+    for name in REST:
+        copy_of(name).wait_recv()
 
     page = c // 16
     columns = pl.ds(pl.multiple_of(h * DH, DH), DH)
@@ -188,10 +330,15 @@
             copy.wait()
 
 
-def attend_kernel(q_ref, seg_ref, kin_ref, vin_ref, buf, out_ref, kc_ref, vc_ref, qx, acc, peak, state):
+def attend_kernel(seg_ref, kin_ref, vin_ref, buf, qx, sums, peaks, out_ref, kc_ref, vc_ref, acc, peak, state):
     c = lax.axis_index("ctx")
+    y, mine = c // 16, c // 4
     kc_ref[...] = kin_ref[...]
     vc_ref[...] = vin_ref[...]
+    acc[0] = sums[...]
+    peak[...] = peaks[...]
+    state[0] = 0
+    state[1] = 0
 
     seg = seg_ref[...]
     starts = [jnp.int32(0)] + [
@@ -203,7 +350,6 @@
     for s in range(4):
         low = jnp.where(lane == s, starts[s], low)
         high = jnp.where(lane == s, starts[s + 1], high)
-    used = jnp.where(lane < 4, 1.0, 0.0)
 
     def inside(first, rows):
         at = lax.broadcasted_iota(jnp.int32, (rows, DH), 0) + first
@@ -215,27 +361,18 @@
             begin = jnp.where(start <= at, start, begin)
         return begin
 
-    own, first_block, inner = [], [], []
+    first, inner = [], []
     for s in range(2):
         at = s * CTX * ROWS + c * ROWS
-        own.append(at // KEYS)
-        first_block.append(segment_start(at) // KEYS)
+        first.append(segment_start(at) // KEYS)
         inner.append(segment_start(at + ROWS - 1))
-    count = own[0] - first_block[0] + 1
-    total = count + own[1] - first_block[1] + 1
-
-    for s in range(2):
-        feature = ((used - inside(s * CTX * ROWS + c * ROWS, ROWS)) * OTHER).astype(jnp.bfloat16)
-        for g in range(GROUPS):
-            qx[s, g, :, :DH] = q_ref[s, :, g * DH : (g + 1) * DH]
-            qx[s, g, :, DH:] = feature
-    peak[...] = jnp.full(peak.shape, START, jnp.float32)
-    acc[0] = jnp.zeros(acc.shape[1:], jnp.float32)
-    state[0] = 0
-    state[1] = 0
+    count = jnp.where(y == 1, jnp.maximum(4 - first[0], 0), 0)
+    upper_first = jnp.maximum(first[1], 4 + 4 * y)
+    upper_count = jnp.maximum(8 + 4 * y - upper_first, 0)
+    total = count + upper_count + jnp.where(first[1] <= mine, 1, 0)
 
     rows = TILE * ROWS
-    lanes = KEYS // DH
+    every = GROUPS * ROWS
     ones = jnp.ones((KEYS, DH), jnp.bfloat16)
 
     def operands(block, featured):
@@ -246,84 +383,62 @@
             keys = jnp.concatenate([keys, inside(block * KEYS, KEYS).astype(jnp.bfloat16)], axis=1)
         return keys, values
 
-    def scores_of(qs, t, keys):
-        width = keys.shape[1]
-        queries = qx[qs, pl.ds(t * TILE, TILE), :, :width].reshape(rows, width)
-        return lax.dot_general(queries, keys, (((1,), (1,)), ((), ())), preferred_element_type=jnp.float32)
-
-    tiles = GROUPS // TILE
-
     def attend(qs, block):
         keys, values = operands(block, True)
+        values = jnp.concatenate([values, ones], axis=1)
         now = state[qs]
-        at = c * ROWS + qs * CTX * ROWS - block * KEYS
-        key_row = lax.broadcasted_iota(jnp.int32, (KEYS, DH), 0)
-        values = jnp.where(key_row < at + ROWS, values, jnp.zeros_like(values))
-        values = jnp.concatenate([values, ones], axis=1)
-        row = lax.broadcasted_iota(jnp.int32, (ROWS, KEYS), 0) + at
-        col = lax.broadcasted_iota(jnp.int32, (ROWS, KEYS), 1)
-        seen = jnp.concatenate([row >= col] * TILE, axis=0)
-        scores = scores_of(qs, 0, keys)
-        for t in range(tiles):
-            later = scores_of(qs, t + 1, keys) if t + 1 < tiles else None
+        for t in range(GROUPS // TILE):
             heads = pl.ds(t * TILE, TILE)
-            scores = jnp.where(seen, scores, LATER)
-            parts = [scores[:, i * DH : (i + 1) * DH] for i in range(lanes)]
-            top = parts[0]
-            for part in parts[1:]:
-                top = jnp.maximum(top, part)
+            queries = qx[qs, heads].reshape(rows, 2 * DH)
+            scores = lax.dot_general(
+                queries, keys, (((1,), (1,)), ((), ())), preferred_element_type=jnp.float32
+            )
             old = peak[qs, heads].reshape(rows, DH)
-            new = jnp.maximum(old, jnp.max(top, axis=1, keepdims=True))
-            weights = jnp.concatenate(
-                [jnp.exp((part - new) * SCALE).astype(jnp.bfloat16) for part in parts], axis=1
-            )
-            factor = jnp.exp((old - new) * SCALE)
-            product = jnp.dot(weights, values, preferred_element_type=jnp.float32)
             held = acc[now, qs, heads].reshape(rows, 2 * DH)
-            held = held * jnp.concatenate([factor, factor], axis=1) + product
+            new, held = online(scores, old, held, values)
             acc[now, qs, heads] = held.reshape(TILE, ROWS, 2 * DH)
             peak[qs, heads] = new.reshape(TILE, ROWS, DH)
-            scores = later
 
     def attend_kept(qs, block, featured):
         keys, values = operands(block, featured)
         values = jnp.concatenate([values, ones], axis=1)
         now = state[qs]
-        scores = scores_of(qs, 0, keys)
-        largest = jnp.zeros((8, DH), jnp.float32)
-        for t in range(tiles):
-            later = scores_of(qs, t + 1, keys) if t + 1 < tiles else None
-            heads = pl.ds(t * TILE, TILE)
-            top = peak[qs, heads].reshape(rows, DH)
-            weights = jnp.concatenate(
-                [
-                    jnp.exp((scores[:, i * DH : (i + 1) * DH] - top) * SCALE).astype(jnp.bfloat16)
-                    for i in range(lanes)
-                ],
-                axis=1,
+        width = keys.shape[1]
+        queries = qx[qs, :, :, :width].reshape(every, width)
+        top = peak[qs].reshape(every, DH)
+
+        def scores_of(i):
+            part = keys[i * 2 * DH : (i + 1) * 2 * DH]
+            return lax.dot_general(
+                queries, part, (((1,), (1,)), ((), ())), preferred_element_type=jnp.float32
             )
-            product = jnp.dot(weights, values, preferred_element_type=jnp.float32)
-            held = acc[now, qs, heads].reshape(rows, 2 * DH) + product
-            acc[1 - now, qs, heads] = held.reshape(TILE, ROWS, 2 * DH)
-            largest = jnp.maximum(largest, jnp.max(held[:, DH:].reshape(rows // 8, 8, DH), axis=0))
+
+        pieces = KEYS // (2 * DH)
+        weights = []
+        scores = scores_of(0)
+        for i in range(pieces):
+            later = scores_of(i + 1) if i + 1 < pieces else None
+            for half in (scores[:, :DH], scores[:, DH:]):
+                weights.append(jnp.exp((half - top) * SCALE).astype(jnp.bfloat16))
             scores = later
-        fits = jnp.max(largest) <= LARGEST
+        product = jnp.dot(jnp.concatenate(weights, axis=1), values, preferred_element_type=jnp.float32)
+        held = acc[now, qs].reshape(every, 2 * DH) + product
+        acc[1 - now, qs] = held.reshape(GROUPS, ROWS, 2 * DH)
+        fits = jnp.max(jnp.max(held[:, DH:].reshape(every // 8, 8, DH), axis=0)) <= LARGEST
         state[qs] = jnp.where(fits, 1 - now, now)
         state[2] = jnp.where(fits, 0, 1)
 
     def step(j, carry):
         upper = j >= count
         qs = jnp.where(upper, 1, 0)
-        mine = jnp.where(upper, own[1], own[0])
-        block = mine - jnp.where(upper, j - count, j)
+        block = jnp.where(upper, jnp.where(j - count < upper_count, upper_first + j - count, mine), first[0] + j)
         plain = block * KEYS >= jnp.where(upper, inner[1], inner[0])
-        state[2] = jnp.where(block == mine, 1, 0)
-
-        @pl.when(jnp.logical_and(block < mine, plain))
+
+        @pl.when(plain)
         def _():
             attend_kept(qs, block, False)
 
-        @pl.when(jnp.logical_and(block < mine, jnp.logical_not(plain)))
+        @pl.when(jnp.logical_not(plain))
         def _():
             attend_kept(qs, block, True)
 
@@ -348,37 +463,44 @@
     vmem = pl.BlockSpec(memory_space=pltpu.VMEM)
     anywhere = pl.BlockSpec(memory_space=pl.ANY)
     cache = jax.ShapeDtypeStruct((CACHE, HEAD * DH), jnp.bfloat16)
-    gathered, keys, values = pl.pallas_call(
+    segments = segment_ids.reshape(-1, DH)
+    gathered, keys, values, prepared, sums, peaks = pl.pallas_call(
         gather_kernel,
-        out_shape=(jax.ShapeDtypeStruct((4, CTX, ROWS, DH), jnp.bfloat16), cache, cache),
-        in_specs=[anywhere] * 2,
-        out_specs=(anywhere,) * 3,
+        out_shape=(
+            jax.ShapeDtypeStruct((4, CTX, ROWS, DH), jnp.bfloat16),
+            cache,
+            cache,
+            jax.ShapeDtypeStruct((2, GROUPS, ROWS, 2 * DH), jnp.bfloat16),
+            jax.ShapeDtypeStruct((2, GROUPS, ROWS, 2 * DH), jnp.float32),
+            jax.ShapeDtypeStruct((2, GROUPS, ROWS, DH), jnp.float32),
+        ),
+        in_specs=[vmem] * 4,
+        out_specs=(vmem, anywhere, anywhere, vmem, vmem, vmem),
         scratch_shapes=[
             pltpu.SemaphoreType.DMA((1,)),
             pltpu.SemaphoreType.DMA((len(TRANSFERS),)),
             pltpu.SemaphoreType.DMA((2, HEAD)),
             pltpu.SemaphoreType.DMA((2, HEAD)),
-            pltpu.SemaphoreType.DMA((4,)),
+            pltpu.SemaphoreType.DMA((2,)),
         ],
         compiler_params=pltpu.CompilerParams(
             collective_id=0, has_side_effects=True, vmem_limit_bytes=GATHER_VMEM
         ),
         name="gather",
-    )(key_states, value_states)
+    )(queries, key_states, value_states, segments)
     return pl.pallas_call(
         attend_kernel,
         out_shape=(jax.ShapeDtypeStruct((2, ROWS, GROUPS * DH), jnp.bfloat16), cache, cache),
-        in_specs=[vmem] * 5,
+        in_specs=[vmem] * 7,
         out_specs=(vmem,) * 3,
         scratch_shapes=[
-            pltpu.VMEM((2, GROUPS, ROWS, 2 * DH), jnp.bfloat16),
             pltpu.VMEM((2, 2, GROUPS, ROWS, 2 * DH), jnp.float32),
             pltpu.VMEM((2, GROUPS, ROWS, DH), jnp.float32),
             pltpu.SMEM((3,), jnp.int32),
         ],
         compiler_params=pltpu.CompilerParams(vmem_limit_bytes=ATTEND_VMEM),
         name="attend",
-    )(queries, segment_ids.reshape(-1, DH), keys, values, gathered)
+    )(segments, keys, values, gathered, prepared, sums, peaks)
 
 
 def solution(mesh):

time: 76.1 us -> 66.5 us (0.87)
  the two profiles are of different devices: /device:TPU:56 before, /device:TPU:24 now
where the time goes in v7:
time: 66.5 us; the launch traced here: 66.2 us
  Pallas kernels  61.9 us (93%)
  local copies, waits for them, and re-layouts  3.71 us (6%)
    pallas_call x1, Pallas kernels, body(): pl.pallas_call(gather_kernel, out_shape=(jax.ShapeDtypeStruct((4, CTX, RO...  46.9 us
    pallas_call x1, Pallas kernels, body(): pl.pallas_call(attend_kernel, out_shape=(jax.ShapeDtypeStruct((2, ROWS, G...  15 us
    unnamed x8, local copies, waits for them, and re-layouts  3.71 us

profile of v7, /device:TPU:24, one launch (start us, length us, event | category | flops | bytes accessed | tf_op | source)
XLA Modules:
  0.0 66.2 jit_solution(2942170079909352847)
XLA Ops:
  0.6 0.0 copy-start
  0.6 1.1 %copy-done = bf16[2,192,1024]{2,1,0:T(8,128)(2,1)S(1)} copy-done((bf16[2,192,1024]{2,1,0:T(8,128)(2,1)S(1)}, bf16[2,192,1024]{2,1,0:T(8,128)(2,1)}, u32[]{:S(2)}) %copy-start) | copy-done | bytes 786456
  1.8 0.0 copy-start.1
  1.8 0.8 %copy-done.1 = s32[12288]{0:T(1024)S(1)} copy-done((s32[12288]{0:T(1024)S(1)}, s32[12288]{0:T(1024)}, u32[]{:S(2)}) %copy-start.1) | copy-done | bytes 49176
  2.6 0.0 copy-start.2
  2.6 0.9 %copy-done.2 = bf16[2,192,128]{2,1,0:T(8,128)(2,1)S(1)} copy-done((bf16[2,192,128]{2,1,0:T(8,128)(2,1)S(1)}, bf16[2,192,128]{2,1,0:T(8,128)(2,1)}, u32[]{:S(2)}) %copy-start.2) | copy-done | bytes 98328
  3.5 0.0 copy-start.3
  3.5 0.9 %copy-done.3 = bf16[2,192,128]{2,1,0:T(8,128)(2,1)S(1)} copy-done((bf16[2,192,128]{2,1,0:T(8,128)(2,1)S(1)}, bf16[2,192,128]{2,1,0:T(8,128)(2,1)}, u32[]{:S(2)}) %copy-start.3) | copy-done | bytes 98328
  4.4 46.9 %gather.1 = (bf16[4,32,192,128]{3,2,1,0:T(8,128)(2,1)S(1)}, bf16[48,1024]{1,0:T(8,128)(2,1)S(1)}, bf16[48,1024]{1,0:T(8,128)(2,1)S(1)}, bf16[2,8,192,256]{3,2,1,...) custom-call(bf16[2,192,1024]{2,1,0:T(8,128)(2,1)S(1)} %copy-done, ...), custom_call_target="tpu_custom_call" | custom-call | tf_op jit(solution)/shard_map/gather/pallas_call | solution.py:467
  51.2 15.0 %attend.1 = (bf16[2,192,1024]{2,1,0:T(8,128)(2,1)}, bf16[48,1024]{1,0:T(8,128)(2,1)}, bf16[48,1024]{1,0:T(8,128)(2,1)}) custom-call(s32[96,128]{1,0:T(8,128)S(1)} %bitcast.2, bf16[48,1024]{1,0:T(8,128)(2,1)S(1)} %get-tuple-element.9.kin_ref, bf16[48,1024]{1,0:T(8,128)(2,1)S(1)} %get-tuple-element.10.vin_ref, ...), custom_call_target="tpu_custom_call" | custom-call | tf_op jit(solution)/shard_map/attend/pallas_call | solution.py:491
Async XLA Ops:
  0.6 1.1 %copy-start = (bf16[2,192,1024]{2,1,0:T(8,128)(2,1)S(1)}, bf16[2,192,1024]{2,1,0:T(8,128)(2,1)}, u32[]{:S(2)}) copy-start(bf16[2,192,1024]{2,1,0:T(8,128)(2,1)} %q_ref.1) | copy-start | bytes 2359300
  1.8 0.8 %copy-start.1 = (s32[12288]{0:T(1024)S(1)}, s32[12288]{0:T(1024)}, u32[]{:S(2)}) copy-start(s32[12288]{0:T(1024)} %param.7) | copy-start | bytes 147460
  2.6 0.9 %copy-start.2 = (bf16[2,192,128]{2,1,0:T(8,128)(2,1)S(1)}, bf16[2,192,128]{2,1,0:T(8,128)(2,1)}, u32[]{:S(2)}) copy-start(bf16[2,192,128]{2,1,0:T(8,128)(2,1)} %k_ref.1) | copy-start | bytes 294916
  3.5 0.9 %copy-start.3 = (bf16[2,192,128]{2,1,0:T(8,128)(2,1)S(1)}, bf16[2,192,128]{2,1,0:T(8,128)(2,1)}, u32[]{:S(2)}) copy-start(bf16[2,192,128]{2,1,0:T(8,128)(2,1)} %v_ref.1) | copy-start | bytes 294916

commit v8 on v7

--- a/solution.py
+++ b/solution.py
@@ -82,20 +82,26 @@
 LATE, LATE_AFTER = [f"{n}{p}" for p in PIECES for n in ("YU1H", "YD1H")], 5
 
 OWN, NEAR, FAR, OPP = 0, 1, 2, 3
-PLAN = [2, 3, (NEAR, LOW), (NEAR, HIGH), 4, 5, (FAR, LOW), (FAR, HIGH), 6, 7, (OPP, LOW), (OPP, HIGH)]
+HALVES = 2
+PLAN = [
+    0, 1, (OWN, 0, LOW), 2, (OWN, 0, LOW), (OWN, 0, HIGH), 3, (OWN, 0, HIGH), (NEAR, 0, LOW), 4, (NEAR, 0, LOW),
+    (NEAR, 0, HIGH), 5, (NEAR, 0, HIGH), (OWN, 1, LOW), (OWN, 1, LOW), 6, (FAR, 0, LOW), (FAR, 0, LOW), 7,
+    (FAR, 0, HIGH), (FAR, 0, HIGH), (NEAR, 1, LOW), 8, (NEAR, 1, LOW), (OPP, 0, LOW), (OPP, 0, LOW),
+    (OPP, 0, HIGH), 9, (OPP, 0, HIGH), (FAR, 1, LOW), (FAR, 1, LOW),
+]
 REACH = {OWN: (0, 1), NEAR: (1, 2), FAR: (2, 3), OPP: (3, 4)}
 
 
-def needs(kind, half):
+def needs(kind, row, half):
     return [
         name
         for name, (link, r, dz, hf, _, _) in TRANSFERS.items()
-        if link == "core" and r == 0 and hf == half and abs(dz) in REACH[kind]
+        if link == "core" and r == row and hf == half and abs(dz) in REACH[kind]
     ]
 
 
 def steps_of(plan):
-    jobs, before, pending, seen = [], [], [], set(needs(OWN, LOW) + needs(OWN, HIGH))
+    jobs, before, pending, seen = [], [], [], set()
     for entry in plan:
         if isinstance(entry, int):
             pending.append(entry)
@@ -105,6 +111,7 @@
             seen.update(fresh)
             before.append((pending, fresh))
             pending = []
+    assert not pending and all(jobs[i] == jobs[i + 1] for i in range(0, len(jobs), HALVES))
     rest = [name for name in TRANSFERS if TRANSFERS[name][0] == "core" and name not in seen]
     return jobs, before, rest
 
@@ -124,7 +131,7 @@
     return new, held * jnp.concatenate([factor, factor], axis=1) + product
 
 
-def gather_kernel(q_ref, k_ref, v_ref, seg_ref, buf, kc_ref, vc_ref, qx, acc, peak, send, recv, csend, crecv, own):
+def gather_kernel(q_ref, k_ref, v_ref, seg_ref, buf, kc_ref, vc_ref, qx, acc, peak, feature, send, recv, csend, crecv, own):
     c = lax.axis_index("ctx")
     h = lax.axis_index("head")
     y, z, core = c // 16, (c % 16) // 2, c % 2
@@ -196,68 +203,52 @@
         return jnp.where((at >= low) & (at < high), 1.0, 0.0)
 
     for s in range(2):
-        feature = ((used - inside(s * CTX * ROWS + c * ROWS, ROWS)) * OTHER).astype(jnp.bfloat16)
+        outside = ((used - inside(s * CTX * ROWS + c * ROWS, ROWS)) * OTHER).astype(jnp.bfloat16)
         for g in range(GROUPS):
             qx[s, g, :, :DH] = q_ref[s, :, g * DH : (g + 1) * DH]
-            qx[s, g, :, DH:] = feature
+            qx[s, g, :, DH:] = outside
     peak[...] = jnp.full(peak.shape, START, jnp.float32)
     acc[...] = jnp.zeros(acc.shape, jnp.float32)
 
     rows = TILE * ROWS
     ones = jnp.ones((KEYS, DH), jnp.bfloat16)
 
-    def attend(qs, half, block, causal):
+    def attend(qs, half, block, part):
         first = block * 4
         keys = buf[2 * half, pl.ds(first, 4)].reshape(KEYS, DH)
         values = buf[2 * half + 1, pl.ds(first, 4)].reshape(KEYS, DH)
-        features = inside((half * CTX + first) * ROWS, KEYS).astype(jnp.bfloat16)
-        keys = jnp.concatenate([keys, features], axis=1)
+
+        @pl.when(part == 0)
+        def _():
+            feature[...] = inside((half * CTX + first) * ROWS, KEYS).astype(jnp.bfloat16)
+
+        keys = jnp.concatenate([keys, feature[...]], axis=1)
         values = jnp.concatenate([values, ones], axis=1)
-        seen = None
-        if causal:
-            row = lax.broadcasted_iota(jnp.int32, (ROWS, KEYS), 0) + (c - first) * ROWS
-            col = lax.broadcasted_iota(jnp.int32, (ROWS, KEYS), 1)
-            seen = jnp.concatenate([row >= col] * TILE, axis=0)
-
-        def scores_of(t):
-            queries = qx[qs, pl.ds(t * TILE, TILE)].reshape(rows, 2 * DH)
-            return lax.dot_general(
-                queries, keys, (((1,), (1,)), ((), ())), preferred_element_type=jnp.float32
-            )
-
-        scores = scores_of(0)
-        for t in range(GROUPS // TILE):
-            later = scores_of(t + 1) if t + 1 < GROUPS // TILE else None
-            heads = pl.ds(t * TILE, TILE)
-            if causal:
-                scores = jnp.where(seen, scores, LATER)
-            old = peak[qs, heads].reshape(rows, DH)
-            held = acc[qs, heads].reshape(rows, 2 * DH)
-            new, held = online(scores, old, held, values)
-            acc[qs, heads] = held.reshape(TILE, ROWS, 2 * DH)
-            peak[qs, heads] = new.reshape(TILE, ROWS, DH)
-            scores = later
+        at = (qs * CTX + c - half * CTX - first) * ROWS
+        row = lax.broadcasted_iota(jnp.int32, (ROWS, KEYS), 0) + at
+        col = lax.broadcasted_iota(jnp.int32, (ROWS, KEYS), 1)
+        seen = jnp.concatenate([row >= col] * TILE, axis=0)
+        heads = pl.ds(part * TILE, TILE)
+        queries = qx[qs, heads].reshape(rows, 2 * DH)
+        scores = lax.dot_general(
+            queries, keys, (((1,), (1,)), ((), ())), preferred_element_type=jnp.float32
+        )
+        scores = jnp.where(seen, scores, LATER)
+        old = peak[qs, heads].reshape(rows, DH)
+        held = acc[qs, heads].reshape(rows, 2 * DH)
+        new, held = online(scores, old, held, values)
+        acc[qs, heads] = held.reshape(TILE, ROWS, 2 * DH)
+        peak[qs, heads] = new.reshape(TILE, ROWS, DH)
 
     zb = z // 2
     mine = y * 4 + zb
     toward = 1 - 2 * (z % 2)
-
-    arrive(0)
-    arrive(1)
-    for name in needs(OWN, LOW) + needs(OWN, HIGH):
-        copy_of(name).wait_recv()
-
-    def own_step(half, carry):
-        attend(half, half, mine, True)
-        return carry
-
-    lax.fori_loop(0, 2, own_step, 0)
 
     def step_body(step, carry):
         def pick(values):
             value = jnp.int32(values[0])
             for i in range(1, len(values)):
-                value = jnp.where(step == i, jnp.int32(values[i]), value)
+                value = jnp.where(job == i, jnp.int32(values[i]), value)
             return value
 
         for i, (events, names) in enumerate(BEFORE):
@@ -270,22 +261,23 @@
                     for name in names:
                         copy_of(name).wait_recv()
 
-        half = pick([job[1] for job in JOBS])
-        move = pick([{NEAR: 0, FAR: 0, OPP: 2}[job[0]] for job in JOBS]) + toward * pick(
-            [{NEAR: -1, FAR: 1, OPP: 0}[job[0]] for job in JOBS]
+        job, part = step // HALVES, step % HALVES
+        jobs = JOBS[::HALVES]
+        row = pick([entry[1] for entry in jobs])
+        half = pick([entry[2] for entry in jobs])
+        move = pick([{OWN: 0, NEAR: 0, FAR: 0, OPP: 2}[entry[0]] for entry in jobs]) + toward * pick(
+            [{OWN: 0, NEAR: -1, FAR: 1, OPP: 0}[entry[0]] for entry in jobs]
         )
-        block = y * 4 + (zb + move + 4) % 4
+        block = jnp.where(row == 0, y, 1 - y) * 4 + (zb + move + 4) % 4
         qs = jnp.where(jnp.logical_or(half == 1, block > mine), 1, 0)
 
-        @pl.when(jnp.logical_or(half == 0, block < mine))
+        @pl.when(jnp.logical_or(half == 0, block <= mine))
         def _():
-            attend(qs, half, block, False)
+            attend(qs, half, block, part)
 
         return carry
 
     lax.fori_loop(0, len(JOBS), step_body, 0)
-    arrive(8)
-    arrive(9)
     for name in REST:
         copy_of(name).wait_recv()
 
@@ -366,10 +358,11 @@
         at = s * CTX * ROWS + c * ROWS
         first.append(segment_start(at) // KEYS)
         inner.append(segment_start(at + ROWS - 1))
-    count = jnp.where(y == 1, jnp.maximum(4 - first[0], 0), 0)
-    upper_first = jnp.maximum(first[1], 4 + 4 * y)
-    upper_count = jnp.maximum(8 + 4 * y - upper_first, 0)
-    total = count + upper_count + jnp.where(first[1] <= mine, 1, 0)
+    opposite = (1 - y) * 4 + (mine + 2) % 4
+    count = jnp.where(jnp.where(y == 1, first[0], first[1]) <= opposite, 1, 0)
+    high_first = jnp.maximum(first[1], 8)
+    high_count = jnp.where(y == 1, jnp.maximum(12 - high_first, 0), 0)
+    total = count + high_count + jnp.where(first[1] <= mine, 1, 0)
 
     rows = TILE * ROWS
     every = GROUPS * ROWS
@@ -429,9 +422,10 @@
         state[2] = jnp.where(fits, 0, 1)
 
     def step(j, carry):
-        upper = j >= count
+        upper = jnp.logical_or(j >= count, y == 0)
         qs = jnp.where(upper, 1, 0)
-        block = jnp.where(upper, jnp.where(j - count < upper_count, upper_first + j - count, mine), first[0] + j)
+        high = j - count
+        block = jnp.where(high < 0, opposite, jnp.where(high < high_count, high_first + high, mine))
         plain = block * KEYS >= jnp.where(upper, inner[1], inner[0])
 
         @pl.when(plain)
@@ -477,6 +471,7 @@
         in_specs=[vmem] * 4,
         out_specs=(vmem, anywhere, anywhere, vmem, vmem, vmem),
         scratch_shapes=[
+            pltpu.VMEM((KEYS, DH), jnp.bfloat16),
             pltpu.SemaphoreType.DMA((1,)),
             pltpu.SemaphoreType.DMA((len(TRANSFERS),)),
             pltpu.SemaphoreType.DMA((2, HEAD)),

time: 66.5 us -> 71.4 us (1.074)
  the two profiles are of different devices: /device:TPU:24 before, /device:TPU:184 now
where the time goes in v8:
time: 71.4 us; the launch traced here: 71.1 us
  Pallas kernels  66.8 us (94%)
  local copies, waits for them, and re-layouts  3.71 us (5%)
    pallas_call x1, Pallas kernels, body(): pl.pallas_call(gather_kernel, out_shape=(jax.ShapeDtypeStruct((4, CTX, RO...  56.9 us
    pallas_call x1, Pallas kernels, body(): pl.pallas_call(attend_kernel, out_shape=(jax.ShapeDtypeStruct((2, ROWS, G...  9.92 us
    unnamed x8, local copies, waits for them, and re-layouts  3.71 us

profile of v8, /device:TPU:184, one launch (start us, length us, event | category | flops | bytes accessed | tf_op | source)
XLA Modules:
  0.0 71.1 jit_solution(2906344916387867109)
XLA Ops:
  0.6 0.0 copy-start
  0.6 1.1 %copy-done = bf16[2,192,1024]{2,1,0:T(8,128)(2,1)S(1)} copy-done((bf16[2,192,1024]{2,1,0:T(8,128)(2,1)S(1)}, bf16[2,192,1024]{2,1,0:T(8,128)(2,1)}, u32[]{:S(2)}) %copy-start) | copy-done | bytes 786456
  1.8 0.0 copy-start.1
  1.8 0.8 %copy-done.1 = s32[12288]{0:T(1024)S(1)} copy-done((s32[12288]{0:T(1024)S(1)}, s32[12288]{0:T(1024)}, u32[]{:S(2)}) %copy-start.1) | copy-done | bytes 49176
  2.6 0.0 copy-start.2
  2.6 0.9 %copy-done.2 = bf16[2,192,128]{2,1,0:T(8,128)(2,1)S(1)} copy-done((bf16[2,192,128]{2,1,0:T(8,128)(2,1)S(1)}, bf16[2,192,128]{2,1,0:T(8,128)(2,1)}, u32[]{:S(2)}) %copy-start.2) | copy-done | bytes 98328
  3.5 0.0 copy-start.3
  3.5 0.9 %copy-done.3 = bf16[2,192,128]{2,1,0:T(8,128)(2,1)S(1)} copy-done((bf16[2,192,128]{2,1,0:T(8,128)(2,1)S(1)}, bf16[2,192,128]{2,1,0:T(8,128)(2,1)}, u32[]{:S(2)}) %copy-start.3) | copy-done | bytes 98328
  4.4 56.9 %gather.1 = (bf16[4,32,192,128]{3,2,1,0:T(8,128)(2,1)S(1)}, bf16[48,1024]{1,0:T(8,128)(2,1)S(1)}, bf16[48,1024]{1,0:T(8,128)(2,1)S(1)}, bf16[2,8,192,256]{3,2,1,...) custom-call(bf16[2,192,1024]{2,1,0:T(8,128)(2,1)S(1)} %copy-done, ...), custom_call_target="tpu_custom_call" | custom-call | tf_op jit(solution)/shard_map/gather/pallas_call | solution.py:461
  61.2 9.9 %attend.1 = (bf16[2,192,1024]{2,1,0:T(8,128)(2,1)}, bf16[48,1024]{1,0:T(8,128)(2,1)}, bf16[48,1024]{1,0:T(8,128)(2,1)}) custom-call(s32[96,128]{1,0:T(8,128)S(1)} %bitcast.2, bf16[48,1024]{1,0:T(8,128)(2,1)S(1)} %get-tuple-element.9.kin_ref, bf16[48,1024]{1,0:T(8,128)(2,1)S(1)} %get-tuple-element.10.vin_ref, ...), custom_call_target="tpu_custom_call" | custom-call | tf_op jit(solution)/shard_map/attend/pallas_call | solution.py:486
Async XLA Ops:
  0.6 1.1 %copy-start = (bf16[2,192,1024]{2,1,0:T(8,128)(2,1)S(1)}, bf16[2,192,1024]{2,1,0:T(8,128)(2,1)}, u32[]{:S(2)}) copy-start(bf16[2,192,1024]{2,1,0:T(8,128)(2,1)} %q_ref.1) | copy-start | bytes 2359300
  1.8 0.8 %copy-start.1 = (s32[12288]{0:T(1024)S(1)}, s32[12288]{0:T(1024)}, u32[]{:S(2)}) copy-start(s32[12288]{0:T(1024)} %param.7) | copy-start | bytes 147460
  2.6 0.9 %copy-start.2 = (bf16[2,192,128]{2,1,0:T(8,128)(2,1)S(1)}, bf16[2,192,128]{2,1,0:T(8,128)(2,1)}, u32[]{:S(2)}) copy-start(bf16[2,192,128]{2,1,0:T(8,128)(2,1)} %k_ref.1) | copy-start | bytes 294916
  3.5 0.9 %copy-start.3 = (bf16[2,192,128]{2,1,0:T(8,128)(2,1)S(1)}, bf16[2,192,128]{2,1,0:T(8,128)(2,1)}, u32[]{:S(2)}) copy-start(bf16[2,192,128]{2,1,0:T(8,128)(2,1)} %v_ref.1) | copy-start | bytes 294916

commit v9 on v7

--- a/solution.py
+++ b/solution.py
@@ -62,6 +62,7 @@
 
 
 TRANSFERS = transfers()
+SPECIAL = [name for name, entry in TRANSFERS.items() if entry[1] == 1 and entry[3] == HIGH]
 INDEX = {name: i for i, name in enumerate(TRANSFERS)}
 FORWARDS = {name: [k for k, v in TRANSFERS.items() if v[5] == name] for name in TRANSFERS}
 FIRST = [f"{n}{half}{p}" for half in "LH" for p in PIECES for n in ("U1", "D1", "Y0")]
@@ -124,7 +125,7 @@
     return new, held * jnp.concatenate([factor, factor], axis=1) + product
 
 
-def gather_kernel(q_ref, k_ref, v_ref, seg_ref, buf, kc_ref, vc_ref, qx, acc, peak, send, recv, csend, crecv, own):
+def gather_kernel(q_ref, k_ref, v_ref, seg_ref, buf, kc_ref, vc_ref, qx, acc, peak, kfeat, send, recv, csend, crecv, own):
     c = lax.axis_index("ctx")
     h = lax.axis_index("head")
     y, z, core = c // 16, (c % 16) // 2, c % 2
@@ -158,27 +159,39 @@
         return pltpu.make_async_remote_copy(
             src_ref=dst,
             dst_ref=dst,
-            send_sem=send.at[0],
+            send_sem=send.at[1 if name in SPECIAL else 0],
             recv_sem=recv.at[INDEX[name]],
             device_id=(target[link], h),
             device_id_type=MESH,
         )
 
+    def start(name):
+        if name not in SPECIAL:
+            copy_of(name).start()
+        else:
+            pl.when(y == (0 if TRANSFERS[name][0] == "y" else 1))(lambda: copy_of(name).start())
+
+    def wait(name):
+        if name not in SPECIAL:
+            copy_of(name).wait_recv()
+        else:
+            pl.when(y == 1)(lambda: copy_of(name).wait_recv())
+
     for name in FIRST:
-        copy_of(name).start()
+        start(name)
 
     def arrive(event):
         names = [f"{n}{p}" for p in PIECES for n in ARRIVALS[event]]
         for name in names:
-            copy_of(name).wait_recv()
+            wait(name)
             for onward in FORWARDS[name]:
                 if TRANSFERS[onward][0] != "core" and onward not in LATE:
-                    copy_of(onward).start()
+                    start(onward)
         for name in names:
-            copy_of("C" + name).start()
+            start("C" + name)
         if event == LATE_AFTER:
             for name in LATE:
-                copy_of(name).start()
+                start(name)
 
     seg = seg_ref[...]
     lane = lax.broadcasted_iota(jnp.int32, (1, DH), 1)
@@ -200,6 +213,13 @@
         for g in range(GROUPS):
             qx[s, g, :, :DH] = q_ref[s, :, g * DH : (g + 1) * DH]
             qx[s, g, :, DH:] = feature
+
+    def prepare_keys(i, carry):
+        for half in range(2):
+            kfeat[half, i] = inside((half * CTX + y * 16 + i) * ROWS, ROWS).astype(jnp.bfloat16)
+        return carry
+
+    lax.fori_loop(0, 16, prepare_keys, 0)
     peak[...] = jnp.full(peak.shape, START, jnp.float32)
     acc[...] = jnp.zeros(acc.shape, jnp.float32)
 
@@ -210,7 +230,7 @@
         first = block * 4
         keys = buf[2 * half, pl.ds(first, 4)].reshape(KEYS, DH)
         values = buf[2 * half + 1, pl.ds(first, 4)].reshape(KEYS, DH)
-        features = inside((half * CTX + first) * ROWS, KEYS).astype(jnp.bfloat16)
+        features = kfeat[half, pl.ds(first - y * 16, 4)].reshape(KEYS, DH)
         keys = jnp.concatenate([keys, features], axis=1)
         values = jnp.concatenate([values, ones], axis=1)
         seen = None
@@ -287,7 +307,7 @@
     arrive(8)
     arrive(9)
     for name in REST:
-        copy_of(name).wait_recv()
+        wait(name)
 
     page = c // 16
     columns = pl.ds(pl.multiple_of(h * DH, DH), DH)
@@ -319,10 +339,22 @@
     for copy in mine:
         copy.start()
 
-    sent = buf.at[:, pl.ds(0, len(TRANSFERS) // (4 * PARTS))]
-    pltpu.make_async_remote_copy(
-        src_ref=sent, dst_ref=sent, send_sem=send.at[0], recv_sem=recv.at[0], device_id=(core_to, h), device_id_type=MESH
-    ).wait_send()
+    def wait_sent(names, sem):
+        halves = 4 if len(names) * 2 % (4 * PARTS * 2) == 0 else 2
+        sent = buf.at[pl.ds(0, halves), pl.ds(0, len(names) // (halves * PARTS))]
+        pltpu.make_async_remote_copy(
+            src_ref=sent,
+            dst_ref=sent,
+            send_sem=send.at[sem],
+            recv_sem=recv.at[0],
+            device_id=(core_to, h),
+            device_id_type=MESH,
+        ).wait_send()
+
+    wait_sent([name for name in TRANSFERS if name not in SPECIAL], 0)
+    for row in range(2):
+        sent_in_row = [name for name in SPECIAL if (TRANSFERS[name][0] == "y") == (row == 0)]
+        pl.when(y == row)(lambda names=sent_in_row: wait_sent(names, 1))
     for copy in mine:
         copy.wait()
     for d in range(1, HEAD):
@@ -372,7 +404,6 @@
     total = count + upper_count + jnp.where(first[1] <= mine, 1, 0)
 
     rows = TILE * ROWS
-    every = GROUPS * ROWS
     ones = jnp.ones((KEYS, DH), jnp.bfloat16)
 
     def operands(block, featured):
@@ -404,27 +435,29 @@
         values = jnp.concatenate([values, ones], axis=1)
         now = state[qs]
         width = keys.shape[1]
-        queries = qx[qs, :, :, :width].reshape(every, width)
-        top = peak[qs].reshape(every, DH)
-
-        def scores_of(i):
-            part = keys[i * 2 * DH : (i + 1) * 2 * DH]
+
+        def scores_of(t):
+            queries = qx[qs, pl.ds(t * TILE, TILE), :, :width].reshape(rows, width)
             return lax.dot_general(
-                queries, part, (((1,), (1,)), ((), ())), preferred_element_type=jnp.float32
+                queries, keys, (((1,), (1,)), ((), ())), preferred_element_type=jnp.float32
             )
 
-        pieces = KEYS // (2 * DH)
-        weights = []
+        largest = jnp.zeros((8, DH), jnp.float32)
         scores = scores_of(0)
-        for i in range(pieces):
-            later = scores_of(i + 1) if i + 1 < pieces else None
-            for half in (scores[:, :DH], scores[:, DH:]):
-                weights.append(jnp.exp((half - top) * SCALE).astype(jnp.bfloat16))
+        for t in range(GROUPS // TILE):
+            later = scores_of(t + 1) if t + 1 < GROUPS // TILE else None
+            heads = pl.ds(t * TILE, TILE)
+            top = peak[qs, heads].reshape(rows, DH)
+            weights = jnp.concatenate(
+                [jnp.exp((scores[:, i : i + DH] - top) * SCALE).astype(jnp.bfloat16) for i in range(0, KEYS, DH)],
+                axis=1,
+            )
+            product = jnp.dot(weights, values, preferred_element_type=jnp.float32)
+            held = acc[now, qs, heads].reshape(rows, 2 * DH) + product
+            acc[1 - now, qs, heads] = held.reshape(TILE, ROWS, 2 * DH)
+            largest = jnp.maximum(largest, jnp.max(held[:, DH:].reshape(rows // 8, 8, DH), axis=0))
             scores = later
-        product = jnp.dot(jnp.concatenate(weights, axis=1), values, preferred_element_type=jnp.float32)
-        held = acc[now, qs].reshape(every, 2 * DH) + product
-        acc[1 - now, qs] = held.reshape(GROUPS, ROWS, 2 * DH)
-        fits = jnp.max(jnp.max(held[:, DH:].reshape(every // 8, 8, DH), axis=0)) <= LARGEST
+        fits = jnp.max(largest) <= LARGEST
         state[qs] = jnp.where(fits, 1 - now, now)
         state[2] = jnp.where(fits, 0, 1)
 
@@ -477,7 +510,8 @@
         in_specs=[vmem] * 4,
         out_specs=(vmem, anywhere, anywhere, vmem, vmem, vmem),
         scratch_shapes=[
-            pltpu.SemaphoreType.DMA((1,)),
+            pltpu.VMEM((2, 16, ROWS, DH), jnp.bfloat16),
+            pltpu.SemaphoreType.DMA((2,)),
             pltpu.SemaphoreType.DMA((len(TRANSFERS),)),
             pltpu.SemaphoreType.DMA((2, HEAD)),
             pltpu.SemaphoreType.DMA((2, HEAD)),

time: 66.5 us -> 64.7 us (0.973)
  Pallas kernels: 61.9 us -> 59.8 us
    pallas_call x1, Pallas kernels: 15 us -> 13.1 us  [body(): pl.pallas_call(attend_kernel, out_shape=(jax.ShapeDtypeStruct((2, ROWS, G...]
where the time goes in v9:
time: 64.7 us; the launch traced here: 64.2 us
  Pallas kernels  59.8 us (92%)
  local copies, waits for them, and re-layouts  3.71 us (6%)
  between operations  0.65 us (1%)
    pallas_call x1, Pallas kernels, body(): pl.pallas_call(gather_kernel, out_shape=(jax.ShapeDtypeStruct((4, CTX, RO...  46.8 us
    pallas_call x1, Pallas kernels, body(): pl.pallas_call(attend_kernel, out_shape=(jax.ShapeDtypeStruct((2, ROWS, G...  13.1 us
    unnamed x8, local copies, waits for them, and re-layouts  3.71 us

profile of v9, /device:TPU:24, one launch (start us, length us, event | category | flops | bytes accessed | tf_op | source)
XLA Modules:
  0.0 64.2 jit_solution(2798125116988178748)
XLA Ops:
  0.6 0.0 copy-start
  0.6 1.1 %copy-done = bf16[2,192,1024]{2,1,0:T(8,128)(2,1)S(1)} copy-done((bf16[2,192,1024]{2,1,0:T(8,128)(2,1)S(1)}, bf16[2,192,1024]{2,1,0:T(8,128)(2,1)}, u32[]{:S(2)}) %copy-start) | copy-done | bytes 786456
  1.8 0.0 copy-start.1
  1.8 0.8 %copy-done.1 = s32[12288]{0:T(1024)S(1)} copy-done((s32[12288]{0:T(1024)S(1)}, s32[12288]{0:T(1024)}, u32[]{:S(2)}) %copy-start.1) | copy-done | bytes 49176
  2.6 0.0 copy-start.2
  2.6 0.9 %copy-done.2 = bf16[2,192,128]{2,1,0:T(8,128)(2,1)S(1)} copy-done((bf16[2,192,128]{2,1,0:T(8,128)(2,1)S(1)}, bf16[2,192,128]{2,1,0:T(8,128)(2,1)}, u32[]{:S(2)}) %copy-start.2) | copy-done | bytes 98328
  3.5 0.0 copy-start.3
  3.5 0.9 %copy-done.3 = bf16[2,192,128]{2,1,0:T(8,128)(2,1)S(1)} copy-done((bf16[2,192,128]{2,1,0:T(8,128)(2,1)S(1)}, bf16[2,192,128]{2,1,0:T(8,128)(2,1)}, u32[]{:S(2)}) %copy-start.3) | copy-done | bytes 98328
  4.4 46.8 %gather.1 = (bf16[4,32,192,128]{3,2,1,0:T(8,128)(2,1)S(1)}, bf16[48,1024]{1,0:T(8,128)(2,1)S(1)}, bf16[48,1024]{1,0:T(8,128)(2,1)S(1)}, bf16[2,8,192,256]{3,2,1,...) custom-call(bf16[2,192,1024]{2,1,0:T(8,128)(2,1)S(1)} %copy-done, ...), custom_call_target="tpu_custom_call" | custom-call | tf_op jit(solution)/shard_map/gather/pallas_call | solution.py:500
  51.1 13.1 %attend.1 = (bf16[2,192,1024]{2,1,0:T(8,128)(2,1)}, bf16[48,1024]{1,0:T(8,128)(2,1)}, bf16[48,1024]{1,0:T(8,128)(2,1)}) custom-call(s32[96,128]{1,0:T(8,128)S(1)} %bitcast.2, bf16[48,1024]{1,0:T(8,128)(2,1)S(1)} %get-tuple-element.9.kin_ref, bf16[48,1024]{1,0:T(8,128)(2,1)S(1)} %get-tuple-element.10.vin_ref, ...), custom_call_target="tpu_custom_call" | custom-call | tf_op jit(solution)/shard_map/attend/pallas_call | solution.py:525
Async XLA Ops:
  0.6 1.1 %copy-start = (bf16[2,192,1024]{2,1,0:T(8,128)(2,1)S(1)}, bf16[2,192,1024]{2,1,0:T(8,128)(2,1)}, u32[]{:S(2)}) copy-start(bf16[2,192,1024]{2,1,0:T(8,128)(2,1)} %q_ref.1) | copy-start | bytes 2359300
  1.8 0.8 %copy-start.1 = (s32[12288]{0:T(1024)S(1)}, s32[12288]{0:T(1024)}, u32[]{:S(2)}) copy-start(s32[12288]{0:T(1024)} %param.7) | copy-start | bytes 147460
  2.6 0.9 %copy-start.2 = (bf16[2,192,128]{2,1,0:T(8,128)(2,1)S(1)}, bf16[2,192,128]{2,1,0:T(8,128)(2,1)}, u32[]{:S(2)}) copy-start(bf16[2,192,128]{2,1,0:T(8,128)(2,1)} %k_ref.1) | copy-start | bytes 294916
  3.5 0.9 %copy-start.3 = (bf16[2,192,128]{2,1,0:T(8,128)(2,1)S(1)}, bf16[2,192,128]{2,1,0:T(8,128)(2,1)}, u32[]{:S(2)}) copy-start(bf16[2,192,128]{2,1,0:T(8,128)(2,1)} %v_ref.1) | copy-start | bytes 294916

commit v10 on v9

--- a/solution.py
+++ b/solution.py
@@ -83,20 +83,23 @@
 LATE, LATE_AFTER = [f"{n}{p}" for p in PIECES for n in ("YU1H", "YD1H")], 5
 
 OWN, NEAR, FAR, OPP = 0, 1, 2, 3
-PLAN = [2, 3, (NEAR, LOW), (NEAR, HIGH), 4, 5, (FAR, LOW), (FAR, HIGH), 6, 7, (OPP, LOW), (OPP, HIGH)]
+PLAN = [
+    2, 3, (NEAR, 0, LOW), (NEAR, 0, HIGH), 4, 5, (FAR, 0, LOW), (FAR, 0, HIGH), (OWN, 1, LOW), 6, 7,
+    (OPP, 0, LOW), (OPP, 0, HIGH), 8, (NEAR, 1, LOW), 9, (FAR, 1, LOW),
+]
 REACH = {OWN: (0, 1), NEAR: (1, 2), FAR: (2, 3), OPP: (3, 4)}
 
 
-def needs(kind, half):
+def needs(kind, row, half):
     return [
         name
         for name, (link, r, dz, hf, _, _) in TRANSFERS.items()
-        if link == "core" and r == 0 and hf == half and abs(dz) in REACH[kind]
+        if link == "core" and r == row and hf == half and abs(dz) in REACH[kind]
     ]
 
 
 def steps_of(plan):
-    jobs, before, pending, seen = [], [], [], set(needs(OWN, LOW) + needs(OWN, HIGH))
+    jobs, before, pending, seen = [], [], [], set(needs(OWN, 0, LOW) + needs(OWN, 0, HIGH))
     for entry in plan:
         if isinstance(entry, int):
             pending.append(entry)
@@ -215,8 +218,8 @@
             qx[s, g, :, DH:] = feature
 
     def prepare_keys(i, carry):
-        for half in range(2):
-            kfeat[half, i] = inside((half * CTX + y * 16 + i) * ROWS, ROWS).astype(jnp.bfloat16)
+        for place, chunk in enumerate((y * 16, CTX + y * 16, (1 - y) * 16)):
+            kfeat[place, i] = inside((chunk + i) * ROWS, ROWS).astype(jnp.bfloat16)
         return carry
 
     lax.fori_loop(0, 16, prepare_keys, 0)
@@ -230,7 +233,8 @@
         first = block * 4
         keys = buf[2 * half, pl.ds(first, 4)].reshape(KEYS, DH)
         values = buf[2 * half + 1, pl.ds(first, 4)].reshape(KEYS, DH)
-        features = kfeat[half, pl.ds(first - y * 16, 4)].reshape(KEYS, DH)
+        place = jnp.where(half == 1, 1, jnp.where(first // 16 == y, 0, 2))
+        features = kfeat[place, pl.ds(first % 16, 4)].reshape(KEYS, DH)
         keys = jnp.concatenate([keys, features], axis=1)
         values = jnp.concatenate([values, ones], axis=1)
         seen = None
@@ -264,7 +268,7 @@
 
     arrive(0)
     arrive(1)
-    for name in needs(OWN, LOW) + needs(OWN, HIGH):
+    for name in needs(OWN, 0, LOW) + needs(OWN, 0, HIGH):
         copy_of(name).wait_recv()
 
     def own_step(half, carry):
@@ -290,11 +294,12 @@
                     for name in names:
                         copy_of(name).wait_recv()
 
-        half = pick([job[1] for job in JOBS])
-        move = pick([{NEAR: 0, FAR: 0, OPP: 2}[job[0]] for job in JOBS]) + toward * pick(
-            [{NEAR: -1, FAR: 1, OPP: 0}[job[0]] for job in JOBS]
+        row = pick([job[1] for job in JOBS])
+        half = pick([job[2] for job in JOBS])
+        move = pick([{OWN: 0, NEAR: 0, FAR: 0, OPP: 2}[job[0]] for job in JOBS]) + toward * pick(
+            [{OWN: 0, NEAR: -1, FAR: 1, OPP: 0}[job[0]] for job in JOBS]
         )
-        block = y * 4 + (zb + move + 4) % 4
+        block = jnp.where(row == 0, y, 1 - y) * 4 + (zb + move + 4) % 4
         qs = jnp.where(jnp.logical_or(half == 1, block > mine), 1, 0)
 
         @pl.when(jnp.logical_or(half == 0, block < mine))
@@ -304,8 +309,6 @@
         return carry
 
     lax.fori_loop(0, len(JOBS), step_body, 0)
-    arrive(8)
-    arrive(9)
     for name in REST:
         wait(name)
 
@@ -398,10 +401,11 @@
         at = s * CTX * ROWS + c * ROWS
         first.append(segment_start(at) // KEYS)
         inner.append(segment_start(at + ROWS - 1))
-    count = jnp.where(y == 1, jnp.maximum(4 - first[0], 0), 0)
-    upper_first = jnp.maximum(first[1], 4 + 4 * y)
-    upper_count = jnp.maximum(8 + 4 * y - upper_first, 0)
-    total = count + upper_count + jnp.where(first[1] <= mine, 1, 0)
+    opposite = (1 - y) * 4 + (mine + 2) % 4
+    count = jnp.where(jnp.where(y == 1, first[0], first[1]) <= opposite, 1, 0)
+    high_first = jnp.maximum(first[1], 8)
+    high_count = jnp.where(y == 1, jnp.maximum(12 - high_first, 0), 0)
+    total = count + high_count + jnp.where(first[1] <= mine, 1, 0)
 
     rows = TILE * ROWS
     ones = jnp.ones((KEYS, DH), jnp.bfloat16)
@@ -462,9 +466,10 @@
         state[2] = jnp.where(fits, 0, 1)
 
     def step(j, carry):
-        upper = j >= count
+        upper = jnp.logical_or(j >= count, y == 0)
         qs = jnp.where(upper, 1, 0)
-        block = jnp.where(upper, jnp.where(j - count < upper_count, upper_first + j - count, mine), first[0] + j)
+        high = j - count
+        block = jnp.where(high < 0, opposite, jnp.where(high < high_count, high_first + high, mine))
         plain = block * KEYS >= jnp.where(upper, inner[1], inner[0])
 
         @pl.when(plain)
@@ -510,7 +515,7 @@
         in_specs=[vmem] * 4,
         out_specs=(vmem, anywhere, anywhere, vmem, vmem, vmem),
         scratch_shapes=[
-            pltpu.VMEM((2, 16, ROWS, DH), jnp.bfloat16),
+            pltpu.VMEM((3, 16, ROWS, DH), jnp.bfloat16),
             pltpu.SemaphoreType.DMA((2,)),
             pltpu.SemaphoreType.DMA((len(TRANSFERS),)),
             pltpu.SemaphoreType.DMA((2, HEAD)),

time: 64.7 us -> 64 us (0.989)
  the two profiles are of different devices: /device:TPU:24 before, /device:TPU:120 now
where the time goes in v10:
time: 64 us; the launch traced here: 63.7 us
  Pallas kernels  59.4 us (93%)
  local copies, waits for them, and re-layouts  3.71 us (6%)
  between operations  0.65 us (1%)
    pallas_call x1, Pallas kernels, body(): pl.pallas_call(gather_kernel, out_shape=(jax.ShapeDtypeStruct((4, CTX, RO...  48.2 us
    pallas_call x1, Pallas kernels, body(): pl.pallas_call(attend_kernel, out_shape=(jax.ShapeDtypeStruct((2, ROWS, G...  11.2 us
    unnamed x8, local copies, waits for them, and re-layouts  3.71 us

profile of v10, /device:TPU:120, one launch (start us, length us, event | category | flops | bytes accessed | tf_op | source)
XLA Modules:
  0.0 63.7 jit_solution(7775558144973184939)
XLA Ops:
  0.6 0.0 copy-start
  0.6 1.1 %copy-done = bf16[2,192,1024]{2,1,0:T(8,128)(2,1)S(1)} copy-done((bf16[2,192,1024]{2,1,0:T(8,128)(2,1)S(1)}, bf16[2,192,1024]{2,1,0:T(8,128)(2,1)}, u32[]{:S(2)}) %copy-start) | copy-done | bytes 786456
  1.8 0.0 copy-start.1
  1.8 0.8 %copy-done.1 = s32[12288]{0:T(1024)S(1)} copy-done((s32[12288]{0:T(1024)S(1)}, s32[12288]{0:T(1024)}, u32[]{:S(2)}) %copy-start.1) | copy-done | bytes 49176
  2.6 0.0 copy-start.2
  2.6 0.9 %copy-done.2 = bf16[2,192,128]{2,1,0:T(8,128)(2,1)S(1)} copy-done((bf16[2,192,128]{2,1,0:T(8,128)(2,1)S(1)}, bf16[2,192,128]{2,1,0:T(8,128)(2,1)}, u32[]{:S(2)}) %copy-start.2) | copy-done | bytes 98328
  3.5 0.0 copy-start.3
  3.5 0.9 %copy-done.3 = bf16[2,192,128]{2,1,0:T(8,128)(2,1)S(1)} copy-done((bf16[2,192,128]{2,1,0:T(8,128)(2,1)S(1)}, bf16[2,192,128]{2,1,0:T(8,128)(2,1)}, u32[]{:S(2)}) %copy-start.3) | copy-done | bytes 98328
  4.4 48.2 %gather.1 = (bf16[4,32,192,128]{3,2,1,0:T(8,128)(2,1)S(1)}, bf16[48,1024]{1,0:T(8,128)(2,1)S(1)}, bf16[48,1024]{1,0:T(8,128)(2,1)S(1)}, bf16[2,8,192,256]{3,2,1,...) custom-call(bf16[2,192,1024]{2,1,0:T(8,128)(2,1)S(1)} %copy-done, ...), custom_call_target="tpu_custom_call" | custom-call | tf_op jit(solution)/shard_map/gather/pallas_call | solution.py:505
  52.5 11.2 %attend.1 = (bf16[2,192,1024]{2,1,0:T(8,128)(2,1)}, bf16[48,1024]{1,0:T(8,128)(2,1)}, bf16[48,1024]{1,0:T(8,128)(2,1)}) custom-call(s32[96,128]{1,0:T(8,128)S(1)} %bitcast.2, bf16[48,1024]{1,0:T(8,128)(2,1)S(1)} %get-tuple-element.9.kin_ref, bf16[48,1024]{1,0:T(8,128)(2,1)S(1)} %get-tuple-element.10.vin_ref, ...), custom_call_target="tpu_custom_call" | custom-call | tf_op jit(solution)/shard_map/attend/pallas_call | solution.py:530
Async XLA Ops:
  0.6 1.1 %copy-start = (bf16[2,192,1024]{2,1,0:T(8,128)(2,1)S(1)}, bf16[2,192,1024]{2,1,0:T(8,128)(2,1)}, u32[]{:S(2)}) copy-start(bf16[2,192,1024]{2,1,0:T(8,128)(2,1)} %q_ref.1) | copy-start | bytes 2359300
  1.8 0.8 %copy-start.1 = (s32[12288]{0:T(1024)S(1)}, s32[12288]{0:T(1024)}, u32[]{:S(2)}) copy-start(s32[12288]{0:T(1024)} %param.7) | copy-start | bytes 147460
  2.6 0.9 %copy-start.2 = (bf16[2,192,128]{2,1,0:T(8,128)(2,1)S(1)}, bf16[2,192,128]{2,1,0:T(8,128)(2,1)}, u32[]{:S(2)}) copy-start(bf16[2,192,128]{2,1,0:T(8,128)(2,1)} %k_ref.1) | copy-start | bytes 294916
  3.5 0.9 %copy-start.3 = (bf16[2,192,128]{2,1,0:T(8,128)(2,1)S(1)}, bf16[2,192,128]{2,1,0:T(8,128)(2,1)}, u32[]{:S(2)}) copy-start(bf16[2,192,128]{2,1,0:T(8,128)(2,1)} %v_ref.1) | copy-start | bytes 294916

commit v11 on v10

--- a/solution.py
+++ b/solution.py
@@ -84,9 +84,10 @@
 
 OWN, NEAR, FAR, OPP = 0, 1, 2, 3
 PLAN = [
-    2, 3, (NEAR, 0, LOW), (NEAR, 0, HIGH), 4, 5, (FAR, 0, LOW), (FAR, 0, HIGH), (OWN, 1, LOW), 6, 7,
-    (OPP, 0, LOW), (OPP, 0, HIGH), 8, (NEAR, 1, LOW), 9, (FAR, 1, LOW),
+    6, (NEAR, 0, LOW), 7, (NEAR, 0, HIGH), (FAR, 0, LOW), 8, (FAR, 0, HIGH), (OWN, 1, LOW), 9, (OPP, 0, LOW),
+    (OPP, 0, HIGH), (NEAR, 1, LOW), (FAR, 1, LOW),
 ]
+CACHE_AT = 8
 REACH = {OWN: (0, 1), NEAR: (1, 2), FAR: (2, 3), OPP: (3, 4)}
 
 
@@ -266,8 +267,8 @@
     mine = y * 4 + zb
     toward = 1 - 2 * (z % 2)
 
-    arrive(0)
-    arrive(1)
+    for event in range(6):
+        arrive(event)
     for name in needs(OWN, 0, LOW) + needs(OWN, 0, HIGH):
         copy_of(name).wait_recv()
 
@@ -276,41 +277,6 @@
         return carry
 
     lax.fori_loop(0, 2, own_step, 0)
-
-    def step_body(step, carry):
-        def pick(values):
-            value = jnp.int32(values[0])
-            for i in range(1, len(values)):
-                value = jnp.where(step == i, jnp.int32(values[i]), value)
-            return value
-
-        for i, (events, names) in enumerate(BEFORE):
-            if events or names:
-
-                @pl.when(step == i)
-                def _(events=events, names=names):
-                    for event in events:
-                        arrive(event)
-                    for name in names:
-                        copy_of(name).wait_recv()
-
-        row = pick([job[1] for job in JOBS])
-        half = pick([job[2] for job in JOBS])
-        move = pick([{OWN: 0, NEAR: 0, FAR: 0, OPP: 2}[job[0]] for job in JOBS]) + toward * pick(
-            [{OWN: 0, NEAR: -1, FAR: 1, OPP: 0}[job[0]] for job in JOBS]
-        )
-        block = jnp.where(row == 0, y, 1 - y) * 4 + (zb + move + 4) % 4
-        qs = jnp.where(jnp.logical_or(half == 1, block > mine), 1, 0)
-
-        @pl.when(jnp.logical_or(half == 0, block < mine))
-        def _():
-            attend(qs, half, block, False)
-
-        return carry
-
-    lax.fori_loop(0, len(JOBS), step_body, 0)
-    for name in REST:
-        wait(name)
 
     page = c // 16
     columns = pl.ds(pl.multiple_of(h * DH, DH), DH)
@@ -332,15 +298,54 @@
             for kv, ref in ((0, kc_ref), (1, vc_ref))
         ]
 
-    for d in range(1, HEAD):
-        for copy in cache_copies(d):
-            copy.start()
-    mine = [
+    local_copies = [
         pltpu.make_async_copy(cache_source(kv, h), ref.at[:, columns], own.at[kv])
         for kv, ref in ((0, kc_ref), (1, vc_ref))
     ]
-    for copy in mine:
-        copy.start()
+
+    def start_cache():
+        for name in REST:
+            wait(name)
+        for d in range(1, HEAD):
+            for copy in cache_copies(d):
+                copy.start()
+        for copy in local_copies:
+            copy.start()
+
+    def step_body(step, carry):
+        def pick(values):
+            value = jnp.int32(values[0])
+            for i in range(1, len(values)):
+                value = jnp.where(step == i, jnp.int32(values[i]), value)
+            return value
+
+        for i, (events, names) in enumerate(BEFORE):
+            if events or names:
+
+                @pl.when(step == i)
+                def _(events=events, names=names):
+                    for event in events:
+                        arrive(event)
+                    for name in names:
+                        copy_of(name).wait_recv()
+
+        pl.when(step == CACHE_AT)(start_cache)
+
+        row = pick([job[1] for job in JOBS])
+        half = pick([job[2] for job in JOBS])
+        move = pick([{OWN: 0, NEAR: 0, FAR: 0, OPP: 2}[job[0]] for job in JOBS]) + toward * pick(
+            [{OWN: 0, NEAR: -1, FAR: 1, OPP: 0}[job[0]] for job in JOBS]
+        )
+        block = jnp.where(row == 0, y, 1 - y) * 4 + (zb + move + 4) % 4
+        qs = jnp.where(jnp.logical_or(half == 1, block > mine), 1, 0)
+
+        @pl.when(jnp.logical_or(half == 0, block < mine))
+        def _():
+            attend(qs, half, block, False)
+
+        return carry
+
+    lax.fori_loop(0, len(JOBS), step_body, 0)
 
     def wait_sent(names, sem):
         halves = 4 if len(names) * 2 % (4 * PARTS * 2) == 0 else 2
@@ -358,7 +363,7 @@
     for row in range(2):
         sent_in_row = [name for name in SPECIAL if (TRANSFERS[name][0] == "y") == (row == 0)]
         pl.when(y == row)(lambda names=sent_in_row: wait_sent(names, 1))
-    for copy in mine:
+    for copy in local_copies:
         copy.wait()
     for d in range(1, HEAD):
         for copy in cache_copies(d):

time: 64 us -> 62.9 us (0.983)
  the two profiles are of different devices: /device:TPU:120 before, /device:TPU:24 now
where the time goes in v11:
time: 62.9 us; the launch traced here: 62.7 us
  Pallas kernels  58.3 us (93%)
  local copies, waits for them, and re-layouts  3.71 us (6%)
  between operations  0.65 us (1%)
    pallas_call x1, Pallas kernels, body(): pl.pallas_call(gather_kernel, out_shape=(jax.ShapeDtypeStruct((4, CTX, RO...  47.1 us
    pallas_call x1, Pallas kernels, body(): pl.pallas_call(attend_kernel, out_shape=(jax.ShapeDtypeStruct((2, ROWS, G...  11.2 us
    unnamed x8, local copies, waits for them, and re-layouts  3.71 us

profile of v11, /device:TPU:24, one launch (start us, length us, event | category | flops | bytes accessed | tf_op | source)
XLA Modules:
  0.0 62.7 jit_solution(699758197798322971)
XLA Ops:
  0.6 0.0 copy-start
  0.6 1.1 %copy-done = bf16[2,192,1024]{2,1,0:T(8,128)(2,1)S(1)} copy-done((bf16[2,192,1024]{2,1,0:T(8,128)(2,1)S(1)}, bf16[2,192,1024]{2,1,0:T(8,128)(2,1)}, u32[]{:S(2)}) %copy-start) | copy-done | bytes 786456
  1.8 0.0 copy-start.1
  1.8 0.8 %copy-done.1 = s32[12288]{0:T(1024)S(1)} copy-done((s32[12288]{0:T(1024)S(1)}, s32[12288]{0:T(1024)}, u32[]{:S(2)}) %copy-start.1) | copy-done | bytes 49176
  2.6 0.0 copy-start.2
  2.6 0.9 %copy-done.2 = bf16[2,192,128]{2,1,0:T(8,128)(2,1)S(1)} copy-done((bf16[2,192,128]{2,1,0:T(8,128)(2,1)S(1)}, bf16[2,192,128]{2,1,0:T(8,128)(2,1)}, u32[]{:S(2)}) %copy-start.2) | copy-done | bytes 98328
  3.5 0.0 copy-start.3
  3.5 0.9 %copy-done.3 = bf16[2,192,128]{2,1,0:T(8,128)(2,1)S(1)} copy-done((bf16[2,192,128]{2,1,0:T(8,128)(2,1)S(1)}, bf16[2,192,128]{2,1,0:T(8,128)(2,1)}, u32[]{:S(2)}) %copy-start.3) | copy-done | bytes 98328
  4.4 47.1 %gather.1 = (bf16[4,32,192,128]{3,2,1,0:T(8,128)(2,1)S(1)}, bf16[48,1024]{1,0:T(8,128)(2,1)S(1)}, bf16[48,1024]{1,0:T(8,128)(2,1)S(1)}, bf16[2,8,192,256]{3,2,1,...) custom-call(bf16[2,192,1024]{2,1,0:T(8,128)(2,1)S(1)} %copy-done, ...), custom_call_target="tpu_custom_call" | custom-call | tf_op jit(solution)/shard_map/gather/pallas_call | solution.py:510
  51.5 11.2 %attend.1 = (bf16[2,192,1024]{2,1,0:T(8,128)(2,1)}, bf16[48,1024]{1,0:T(8,128)(2,1)}, bf16[48,1024]{1,0:T(8,128)(2,1)}) custom-call(s32[96,128]{1,0:T(8,128)S(1)} %bitcast.2, bf16[48,1024]{1,0:T(8,128)(2,1)S(1)} %get-tuple-element.9.kin_ref, bf16[48,1024]{1,0:T(8,128)(2,1)S(1)} %get-tuple-element.10.vin_ref, ...), custom_call_target="tpu_custom_call" | custom-call | tf_op jit(solution)/shard_map/attend/pallas_call | solution.py:535
Async XLA Ops:
  0.6 1.1 %copy-start = (bf16[2,192,1024]{2,1,0:T(8,128)(2,1)S(1)}, bf16[2,192,1024]{2,1,0:T(8,128)(2,1)}, u32[]{:S(2)}) copy-start(bf16[2,192,1024]{2,1,0:T(8,128)(2,1)} %q_ref.1) | copy-start | bytes 2359300
  1.8 0.8 %copy-start.1 = (s32[12288]{0:T(1024)S(1)}, s32[12288]{0:T(1024)}, u32[]{:S(2)}) copy-start(s32[12288]{0:T(1024)} %param.7) | copy-start | bytes 147460
  2.6 0.9 %copy-start.2 = (bf16[2,192,128]{2,1,0:T(8,128)(2,1)S(1)}, bf16[2,192,128]{2,1,0:T(8,128)(2,1)}, u32[]{:S(2)}) copy-start(bf16[2,192,128]{2,1,0:T(8,128)(2,1)} %k_ref.1) | copy-start | bytes 294916
  3.5 0.9 %copy-start.3 = (bf16[2,192,128]{2,1,0:T(8,128)(2,1)S(1)}, bf16[2,192,128]{2,1,0:T(8,128)(2,1)}, u32[]{:S(2)}) copy-start(bf16[2,192,128]{2,1,0:T(8,128)(2,1)} %v_ref.1) | copy-start | bytes 294916

commit v12 on v11

--- a/solution.py
+++ b/solution.py
@@ -84,10 +84,9 @@
 
 OWN, NEAR, FAR, OPP = 0, 1, 2, 3
 PLAN = [
-    6, (NEAR, 0, LOW), 7, (NEAR, 0, HIGH), (FAR, 0, LOW), 8, (FAR, 0, HIGH), (OWN, 1, LOW), 9, (OPP, 0, LOW),
-    (OPP, 0, HIGH), (NEAR, 1, LOW), (FAR, 1, LOW),
+    6, (NEAR, 0, LOW), 7, (NEAR, 0, HIGH), (FAR, 0, LOW), 8, (FAR, 0, HIGH), 9, (OPP, 0, LOW), (OPP, 0, HIGH),
 ]
-CACHE_AT = 8
+CACHE_AT = 5
 REACH = {OWN: (0, 1), NEAR: (1, 2), FAR: (2, 3), OPP: (3, 4)}
 
 
@@ -406,11 +405,10 @@
         at = s * CTX * ROWS + c * ROWS
         first.append(segment_start(at) // KEYS)
         inner.append(segment_start(at + ROWS - 1))
-    opposite = (1 - y) * 4 + (mine + 2) % 4
-    count = jnp.where(jnp.where(y == 1, first[0], first[1]) <= opposite, 1, 0)
-    high_first = jnp.maximum(first[1], 8)
-    high_count = jnp.where(y == 1, jnp.maximum(12 - high_first, 0), 0)
-    total = count + high_count + jnp.where(first[1] <= mine, 1, 0)
+    count = jnp.where(y == 1, jnp.maximum(4 - first[0], 0), 0)
+    upper_first = jnp.maximum(first[1], 4 + 4 * y)
+    upper_count = jnp.maximum(8 + 4 * y - upper_first, 0)
+    total = count + upper_count + jnp.where(first[1] <= mine, 1, 0)
 
     rows = TILE * ROWS
     ones = jnp.ones((KEYS, DH), jnp.bfloat16)
@@ -471,10 +469,9 @@
         state[2] = jnp.where(fits, 0, 1)
 
     def step(j, carry):
-        upper = jnp.logical_or(j >= count, y == 0)
+        upper = j >= count
         qs = jnp.where(upper, 1, 0)
-        high = j - count
-        block = jnp.where(high < 0, opposite, jnp.where(high < high_count, high_first + high, mine))
+        block = jnp.where(upper, jnp.where(j - count < upper_count, upper_first + j - count, mine), first[0] + j)
         plain = block * KEYS >= jnp.where(upper, inner[1], inner[0])
 
         @pl.when(plain)

time: 62.9 us -> 63.8 us (1.014); the launches traced: 62.7 us -> 64.5 us
  Pallas kernels: 58.3 us -> 60.2 us
    pallas_call x1, Pallas kernels: 11.2 us -> 15 us  [body(): pl.pallas_call(attend_kernel, out_shape=(jax.ShapeDtypeStruct((2, ROWS, G...]
    pallas_call x1, Pallas kernels: 47.1 us -> 45.2 us  [body(): pl.pallas_call(gather_kernel, out_shape=(jax.ShapeDtypeStruct((4, CTX, RO...]
where the time goes in v12:
time: 63.8 us; the launch traced here: 64.5 us
  Pallas kernels  60.2 us (94%)
  local copies, waits for them, and re-layouts  3.71 us (6%)
  between operations  0.65 us (1%)
    pallas_call x1, Pallas kernels, body(): pl.pallas_call(gather_kernel, out_shape=(jax.ShapeDtypeStruct((4, CTX, RO...  45.2 us
    pallas_call x1, Pallas kernels, body(): pl.pallas_call(attend_kernel, out_shape=(jax.ShapeDtypeStruct((2, ROWS, G...  15 us
    unnamed x8, local copies, waits for them, and re-layouts  3.71 us

profile of v12, /device:TPU:24, one launch (start us, length us, event | category | flops | bytes accessed | tf_op | source)
XLA Modules:
  0.0 64.5 jit_solution(6322377611011082974)
XLA Ops:
  0.6 0.0 copy-start
  0.6 1.1 %copy-done = bf16[2,192,1024]{2,1,0:T(8,128)(2,1)S(1)} copy-done((bf16[2,192,1024]{2,1,0:T(8,128)(2,1)S(1)}, bf16[2,192,1024]{2,1,0:T(8,128)(2,1)}, u32[]{:S(2)}) %copy-start) | copy-done | bytes 786456
  1.8 0.0 copy-start.1
  1.8 0.8 %copy-done.1 = s32[12288]{0:T(1024)S(1)} copy-done((s32[12288]{0:T(1024)S(1)}, s32[12288]{0:T(1024)}, u32[]{:S(2)}) %copy-start.1) | copy-done | bytes 49176
  2.6 0.0 copy-start.2
  2.6 0.9 %copy-done.2 = bf16[2,192,128]{2,1,0:T(8,128)(2,1)S(1)} copy-done((bf16[2,192,128]{2,1,0:T(8,128)(2,1)S(1)}, bf16[2,192,128]{2,1,0:T(8,128)(2,1)}, u32[]{:S(2)}) %copy-start.2) | copy-done | bytes 98328
  3.5 0.0 copy-start.3
  3.5 0.9 %copy-done.3 = bf16[2,192,128]{2,1,0:T(8,128)(2,1)S(1)} copy-done((bf16[2,192,128]{2,1,0:T(8,128)(2,1)S(1)}, bf16[2,192,128]{2,1,0:T(8,128)(2,1)}, u32[]{:S(2)}) %copy-start.3) | copy-done | bytes 98328
  4.4 45.2 %gather.1 = (bf16[4,32,192,128]{3,2,1,0:T(8,128)(2,1)S(1)}, bf16[48,1024]{1,0:T(8,128)(2,1)S(1)}, bf16[48,1024]{1,0:T(8,128)(2,1)S(1)}, bf16[2,8,192,256]{3,2,1,...) custom-call(bf16[2,192,1024]{2,1,0:T(8,128)(2,1)S(1)} %copy-done, ...), custom_call_target="tpu_custom_call" | custom-call | tf_op jit(solution)/shard_map/gather/pallas_call | solution.py:507
  49.5 15.0 %attend.1 = (bf16[2,192,1024]{2,1,0:T(8,128)(2,1)}, bf16[48,1024]{1,0:T(8,128)(2,1)}, bf16[48,1024]{1,0:T(8,128)(2,1)}) custom-call(s32[96,128]{1,0:T(8,128)S(1)} %bitcast.2, bf16[48,1024]{1,0:T(8,128)(2,1)S(1)} %get-tuple-element.9.kin_ref, bf16[48,1024]{1,0:T(8,128)(2,1)S(1)} %get-tuple-element.10.vin_ref, ...), custom_call_target="tpu_custom_call" | custom-call | tf_op jit(solution)/shard_map/attend/pallas_call | solution.py:532
Async XLA Ops:
  0.6 1.1 %copy-start = (bf16[2,192,1024]{2,1,0:T(8,128)(2,1)S(1)}, bf16[2,192,1024]{2,1,0:T(8,128)(2,1)}, u32[]{:S(2)}) copy-start(bf16[2,192,1024]{2,1,0:T(8,128)(2,1)} %q_ref.1) | copy-start | bytes 2359300
  1.8 0.8 %copy-start.1 = (s32[12288]{0:T(1024)S(1)}, s32[12288]{0:T(1024)}, u32[]{:S(2)}) copy-start(s32[12288]{0:T(1024)} %param.7) | copy-start | bytes 147460
  2.6 0.9 %copy-start.2 = (bf16[2,192,128]{2,1,0:T(8,128)(2,1)S(1)}, bf16[2,192,128]{2,1,0:T(8,128)(2,1)}, u32[]{:S(2)}) copy-start(bf16[2,192,128]{2,1,0:T(8,128)(2,1)} %k_ref.1) | copy-start | bytes 294916
  3.5 0.9 %copy-start.3 = (bf16[2,192,128]{2,1,0:T(8,128)(2,1)S(1)}, bf16[2,192,128]{2,1,0:T(8,128)(2,1)}, u32[]{:S(2)}) copy-start(bf16[2,192,128]{2,1,0:T(8,128)(2,1)} %v_ref.1) | copy-start | bytes 294916
